TPU v7x, 512 devices: a whole 4x8x8 slice. The times are simulated.
512 devices in a mesh: row: 8 (over x, y_hi), col: 32 (over z, y_lo), rep: 2 (over core).
Axes of the slice: x: 4, y: 8 (y_hi: 2, y_lo: 4; y = y_hi * 4 + y_lo), z: 8, core: 2. Of those that a mesh axis runs over, the one named last changes fastest.
Arguments:
- x_src: bfloat16 [32, 2048, 128], P('col', ('row', 'rep')), may hold values from -6 to 6
- x_dst: bfloat16 [8, 2048, 128], P('row', ('col', 'rep')), may hold values from -6 to 6
- degree: int32 [8, 2048], P('row', ('col', 'rep')), may hold values from 16 to 128
- tile_vals: bfloat16 [8, 32, 2, 24, 256, 256], P('row', 'col', 'rep'), may hold values from -6 to 6
- tile_rows: int32 [8, 32, 2, 24], P('row', 'col', 'rep'), may hold values from 0 to 7
- tile_cols: int32 [8, 32, 2, 24], P('row', 'col', 'rep'), may hold values from 0 to 7
- tile_count: int32 [8, 32, 2], P('row', 'col', 'rep'), may hold values from 1 to 24, as said below
- w_self: bfloat16 [128, 512], replicated, may hold values from -0.5 to 0.5
- w_neigh: bfloat16 [128, 512], replicated, may hold values from -0.5 to 0.5
- cotangent: bfloat16 [8, 2048, 512], P('row', ('col', 'rep')), may hold values from -6 to 6
Outputs:
- hidden: bfloat16 [8, 2048, 512], P('row', ('col', 'rep'))
- d_x_src: bfloat16 [32, 2048, 128], P('col', ('row', 'rep'))
- d_x_dst: bfloat16 [8, 2048, 128], P('row', ('col', 'rep'))
- d_w_self: float32 [128, 512], replicated
- d_w_neigh: float32 [128, 512], replicated
Inputs may be any that keep to these rules, and one draw needn't show every extreme that they name: `tile_count`: live tiles of one device; some device has all 24 slots live in every draw.
All inputs are finite; a program needn't handle non-finite values.
Results may differ from a plain program's by a relative error of at most 0.0072.
Values may be sent and summed in bfloat16 or wider, within the bound.
No kernel may reach another device: no remote copies, remote signals or barrier semaphores. Data moves between devices by JAX's collectives and lax.ppermute only.
A program may use at most 64 MiB of HBM per device.

v0:
```python
import jax
import jax.numpy as jnp
from jax import lax
from jax.sharding import PartitionSpec as P


def gelu_tanh(v):
    return jax.nn.gelu(v, approximate=True)


def on_device(
    x_src, x_dst, degree, tile_vals, tile_rows, tile_cols, tile_count, w_self, w_neigh, cotangent
):
    block = lax.all_gather(x_src, ("row", "rep"), axis=1, tiled=True)[0]
    vals = tile_vals.reshape(tile_vals.shape[3:])
    rows = tile_rows.reshape(-1)
    cols = tile_cols.reshape(-1)
    count = tile_count.reshape(-1)[0]
    tile = vals.shape[-1]
    feat = block.shape[1]
    own_rows = x_dst.shape[1]
    ncol = lax.axis_size("col")
    nrep = lax.axis_size("rep")
    row_block = own_rows * ncol * nrep
    col_block = block.shape[0]
    start = 0

    def fetch(k):
        matrix = lax.dynamic_index_in_dim(vals, k, 0, keepdims=False)
        return (matrix, rows[k], cols[k])

    def forward_step(k, acc):
        matrix, row_tile, col_tile = fetch(k)
        source = lax.dynamic_slice_in_dim(block, col_tile * tile, tile, 0)
        part_sum = jnp.dot(matrix, source, preferred_element_type=jnp.float32)
        current = lax.dynamic_slice_in_dim(acc, row_tile * tile, tile, 0)
        return lax.dynamic_update_slice_in_dim(acc, current + part_sum, row_tile * tile, 0)

    partial_value = lax.fori_loop(
        start, count, forward_step, jnp.zeros((row_block, feat), jnp.float32)
    )
    agg = lax.psum_scatter(partial_value, ("col", "rep"), scatter_dimension=0, tiled=True)
    deg = degree[0].astype(jnp.float32)[:, None]
    neigh = (agg / deg).astype(jnp.bfloat16)
    own_feats = x_dst[0]
    pre = jnp.dot(own_feats, w_self, preferred_element_type=jnp.float32) + jnp.dot(
        neigh, w_neigh, preferred_element_type=jnp.float32
    )
    hidden = gelu_tanh(pre).astype(jnp.bfloat16)
    _, pull = jax.vjp(gelu_tanh, pre)
    dpre = pull(cotangent[0].astype(jnp.float32))[0].astype(jnp.bfloat16)
    grad_self, grad_neigh = lax.psum(
        (
            jnp.dot(own_feats.T, dpre, preferred_element_type=jnp.float32),
            jnp.dot(neigh.T, dpre, preferred_element_type=jnp.float32),
        ),
        ("row", "col", "rep"),
    )
    d_x_dst = jnp.dot(dpre, w_self.T, preferred_element_type=jnp.float32).astype(jnp.bfloat16)
    dagg = (jnp.dot(dpre, w_neigh.T, preferred_element_type=jnp.float32) / deg).astype(jnp.bfloat16)
    grad_block = lax.all_gather(dagg, ("col", "rep"), axis=0, tiled=True)

    def backward_step(k, acc):
        matrix, row_tile, col_tile = fetch(k)
        upstream = lax.dynamic_slice_in_dim(grad_block, row_tile * tile, tile, 0)
        part_sum = lax.dot_general(
            matrix, upstream, (((0,), (0,)), ((), ())), preferred_element_type=jnp.float32
        )
        current = lax.dynamic_slice_in_dim(acc, col_tile * tile, tile, 0)
        return lax.dynamic_update_slice_in_dim(acc, current + part_sum, col_tile * tile, 0)

    back_partial = lax.fori_loop(
        start, count, backward_step, jnp.zeros((col_block, feat), jnp.float32)
    )
    d_x_src = lax.psum_scatter(
        back_partial, ("row", "rep"), scatter_dimension=0, tiled=True
    ).astype(jnp.bfloat16)
    return (hidden[None], d_x_src[None], d_x_dst[None], grad_self, grad_neigh)


def solution(mesh):
    return jax.shard_map(
        on_device,
        mesh=mesh,
        in_specs=(
            P("col", ("row", "rep"), None),
            P("row", ("col", "rep"), None),
            P("row", ("col", "rep")),
            P("row", "col", "rep", None, None, None),
            P("row", "col", "rep", None),
            P("row", "col", "rep", None),
            P("row", "col", "rep"),
            P(),
            P(),
            P("row", ("col", "rep"), None),
        ),
        out_specs=(
            P("row", ("col", "rep"), None),
            P("col", ("row", "rep"), None),
            P("row", ("col", "rep"), None),
            P(),
            P(),
        ),
        check_vma=False,
    )
```

profile of v0, /device:TPU:1, one launch (start us, length us, event | category | flops | bytes accessed | tf_op | source)
XLA Modules:
  0.0 900.6 jit_solution(560114154866583536)
XLA Ops:
  7.2 0.0 copy-start
  7.2 0.0 copy-start.6
  7.2 0.0 copy-start.3
  7.2 0.0 copy-start.4
  7.2 0.0 copy-start.5
  7.2 0.0 reduce-scatter.3.cloned.1.call-start
  7.3 35.9 %all_gather.6 = bf16[1,2048,128]{2,1,0:T(8,128)(2,1)S(1)} all-gather(bf16[1,128,128]{2,1,0:T(8,128)(2,1)} %param.14), channel_id=1, replica_groups=mesh['row'=8,'col'=32,'rep'=2] {'row','rep'}, dimensions={1}, use_global_device_ids=true | all-gather | bytes 557056 | tf_op jit(solution)/shard_map/all_gather | solution.py:14
  43.2 0.1 broadcast.16.clone
  43.3 11.8 %while.20 = (s32[]{:T(128)}, f32[2048,128]{1,0:T(8,128)S(1)}, s32[]{:T(128)}, s32[24]{0:T(128)}, bf16[24,256,256]{2,1,0:T(8,128)(2,1)}, /*index=5*/s32[24]{0:T(1...) while((s32[]{:T(128)}, f32[2048,128]{1,0:T(8,128)S(1)}, ...), condition=%wide.region_1.2_spmd, body=%wide.region_0.1_spmd.sunk | while | flops 16809996 | bytes 459039 | solution.py:39
  43.9 1.2 dynamic_slice.58
  45.8 1.2 dynamic_slice.59
  47.7 1.1 fusion.43
  49.5 1.2 dynamic_slice.58
  51.4 1.2 dynamic_slice.59
  53.3 1.1 fusion.43
  55.1 0.0 copy-start.2
  55.1 0.0 copy-start.7
  55.1 0.0 copy-start.8
  55.1 0.9 copy-done.2
  56.0 0.0 reduce-scatter.3.cloned.1.call-update
  56.1 0.0 all-reduce.3.cloned.1.call-start
  56.2 0.1 fusion.24
  56.3 396.1 %reduce-scatter.3.cloned.1.call-done = f32[32,128]{1,0:T(8,128)} async-done(((f32[2048,128]{1,0:T(8,128)}), f32[32,128]{1,0:T(8,128)}) %reduce-scatter.3.cloned.1.call-update) | async-done | bytes 16400 | tf_op jit(solution)/shard_map/reduce_scatter | solution.py:42
  452.4 1.6 fusion.14
  454.0 0.1 fusion.10
  454.1 0.9 convolution_bitcast_fusion
  455.1 81.8 %all_gather.7 = bf16[2048,128]{1,0:T(8,128)(2,1)S(1)} all-gather(bf16[32,128]{1,0:T(8,128)(2,1)S(1)} %fusion.10), channel_id=1, replica_groups=mesh['row'=8,'col'=32,'rep'=2] {'col','rep'}, dimensions={0}, use_global_device_ids=true | all-gather | bytes 532480 | tf_op jit(solution)/shard_map/all_gather | solution.py:61
  536.8 1.7 fusion.26
  538.5 0.0 all-reduce.3.cloned.1.call-update
  538.6 0.0 reduce-scatter.5.cloned.1.call-start
  538.6 0.1 broadcast.16
  538.7 0.0 copy-done.7
  538.7 0.0 copy-done.8
  538.7 9.2 %while.21 = (s32[]{:T(128)}, f32[2048,128]{1,0:T(8,128)S(1)}, s32[]{:T(128)}, s32[24]{0:T(128)S(1)}, bf16[24,256,256]{2,1,0:T(8,128)(2,1)}, /*index=5*/s32[24]{0...) while((s32[]{:T(128)}, f32[2048,128]{1,0:T(8,128)S(1)}, ...), condition=%wide.region_4.5_spmd, body=%wide.region_3.4_spmd.sunk | while | flops 16809996 | bytes 459039 | solution.py:72
  539.4 0.6 dynamic_slice.63
  540.6 0.6 dynamic_slice.64
  541.9 1.1 fusion.46
  543.7 0.6 dynamic_slice.63
  544.9 0.6 dynamic_slice.64
  546.2 1.1 fusion.46
  548.0 1.0 copy-done.1
  549.0 0.0 reduce-scatter.5.cloned.1.call-update
  549.0 0.8 fusion.11
  549.7 254.0 %all-reduce.3.cloned.1.call-done = (f32[128,512]{0,1:T(8,128)}, f32[128,512]{1,0:T(8,128)}) async-done(((f32[128,512]{0,1:T(8,128)}, f32[128,512]{1,0:T(8,128)}), (f32[128,512]{0,1:T(8,128)}, f32[128,512]{1,0:T(8,128)})) %all-reduce.3.cloned.1.call-update) | async-done | bytes 524304 | tf_op jit(solution)/shard_map/psum | solution.py:52
  803.7 1.8 copy.15
  805.5 85.4 %reduce-scatter.5.cloned.1.call-done = f32[128,128]{1,0:T(8,128)} async-done(((f32[2048,128]{1,0:T(8,128)}), f32[128,128]{1,0:T(8,128)}) %reduce-scatter.5.cloned.1.call-update) | async-done | bytes 65552 | tf_op jit(solution)/shard_map/reduce_scatter | solution.py:75
  890.9 1.5 convert_bitcast_fusion
  892.4 1.7 copy.32
  (7 shorter events, 0.0 us)
Async XLA Ops:
  7.2 445.3 %copy-start = (bf16[128,512]{1,0:T(8,128)(2,1)S(1)}, bf16[128,512]{1,0:T(8,128)(2,1)}, u32[]{:S(2)}) copy-start(bf16[128,512]{1,0:T(8,128)(2,1)} %param.22) | copy-start | bytes 393220
  7.2 48.9 %copy-start.6 = (s32[1,32]{1,0:T(1,128)S(1)}, s32[1,32]{1,0:T(1,128)}, u32[]{:S(2)}) copy-start(s32[1,32]{1,0:T(1,128)} %param.16) | copy-start | bytes 388
  7.2 48.9 %copy-start.3 = (bf16[128,512]{1,0:T(8,128)(2,1)S(1)}, bf16[128,512]{1,0:T(8,128)(2,1)}, u32[]{:S(2)}) copy-start(bf16[128,512]{1,0:T(8,128)(2,1)} %param.21) | copy-start | bytes 393220
  7.2 48.9 %copy-start.4 = (bf16[1,32,128]{2,1,0:T(8,128)(2,1)S(1)}, bf16[1,32,128]{2,1,0:T(8,128)(2,1)}, u32[]{:S(2)}) copy-start(bf16[1,32,128]{2,1,0:T(8,128)(2,1)} %param.15) | copy-start | bytes 24580
  7.2 445.2 %copy-start.5 = (bf16[1,32,512]{2,1,0:T(8,128)(2,1)S(1)}, bf16[1,32,512]{2,1,0:T(8,128)(2,1)}, u32[]{:S(2)}) copy-start(bf16[1,32,512]{2,1,0:T(8,128)(2,1)} %param.23) | copy-start | bytes 98308
  7.2 445.2 %reduce-scatter.3.cloned.1.call-start = ((), (), s32[]{:S(2)}) async-start(), calls=%async_computation.2 | async-start | bytes 1064960 | tf_op jit(solution)/shard_map/reduce_scatter | solution.py:42
  55.1 1.0 copy-start.2
  55.1 483.6 %copy-start.7 = (s32[24]{0:T(128)S(1)}, s32[24]{0:T(128)}, u32[]{:S(2)}) copy-start(s32[24]{0:T(128)} %get-tuple-element.304) | copy-start | bytes 292
  55.1 483.6 %copy-start.8 = (s32[24]{0:T(128)S(1)}, s32[24]{0:T(128)}, u32[]{:S(2)}) copy-start(s32[24]{0:T(128)} %get-tuple-element.305) | copy-start | bytes 292
  56.1 747.7 %all-reduce.3.cloned.1.call-start = ((), (), s32[]{:S(2)}) async-start(), calls=%async_computation.4 | async-start | bytes 1048576 | tf_op jit(solution)/shard_map/psum | solution.py:52
  538.6 352.3 %reduce-scatter.5.cloned.1.call-start = ((), (), s32[]{:S(2)}) async-start(), calls=%async_computation.3 | async-start | bytes 1114112 | tf_op jit(solution)/shard_map/reduce_scatter | solution.py:75
  548.0 1.0 copy-start.1
Sparse Core Ops, SparseCore 0:
  56.2 396.1 reduce-scatter.2
  538.7 264.9 all-reduce.2
  808.4 82.4 reduce-scatter.4
where the time goes:
time: 904 us; the launch traced here: 901 us
  waiting for transfers between devices  736 us (81%)
  blocking collectives  118 us (13%)
  between operations  13.9 us (2%)
  local copies, waits for them, and re-layouts  12.9 us (1%)
  matrix products  9.68 us (1%)
  loops' own time  9.25 us (1%)
    reduce_scatter x1, waiting for transfers between devices, on_device(): lax.psum_scatter(partial_value, ('col', 'rep'), scatter_dimension=0, tile...  396 us
    psum x1, waiting for transfers between devices, on_device(): lax.psum((jnp.dot(own_feats.T, dpre, preferred_element_type=jnp.float32),...  254 us
    reduce_scatter x1, waiting for transfers between devices, on_device(): lax.psum_scatter(back_partial, ('row', 'rep'), scatter_dimension=0, tiled...  85.4 us
    all_gather x1, blocking collectives, on_device(): grad_block = lax.all_gather(dagg, ('col', 'rep'), axis=0, tiled=True)  81.8 us
    all_gather x1, blocking collectives, on_device(): block = lax.all_gather(x_src, ('row', 'rep'), axis=1, tiled=True)[0]  35.9 us
  transfers between devices with their start and end apart: 3, of which 3 were waited for; matrix products, arithmetic and copies ran while one was open for 1% of the time, Pallas kernels for 0%

commit v1 on v0

v1 whole, which is shorter than its diff:
```python
import jax
import jax.numpy as jnp
from jax import lax
from jax.experimental import pallas as pl
from jax.experimental.pallas import tpu as pltpu
from jax.sharding import PartitionSpec as P

GELU_SCALE = 0.7978845608
GELU_CUBE = 0.044715
MIB = 1 << 20
VMEM = pl.BlockSpec(memory_space=pltpu.VMEM)
SMEM = pl.BlockSpec(memory_space=pltpu.SMEM)


def call(kernel, out_shape, operands, in_specs=None, scratch=(), limit=16, cost=None):
    return pl.pallas_call(
        kernel,
        out_shape=out_shape,
        in_specs=in_specs or [VMEM] * len(operands),
        out_specs=jax.tree.map(lambda _: VMEM, out_shape),
        scratch_shapes=list(scratch),
        compiler_params=pltpu.CompilerParams(vmem_limit_bytes=limit * MIB),
        cost_estimate=cost,
    )(*operands)


def forward_kernel(rows, cols, count, core, source, tiles, keep, send, block, acc):
    nrep, nrow, part, _ = source.shape
    tile = tiles.shape[-1]
    own_rows = keep.shape[1]
    for r in range(nrow):
        for c in range(nrep):
            block[pl.ds((r * nrep + c) * part, part), :] = source[c, r]
    acc[...] = jnp.zeros_like(acc)

    def step(k, carry):
        start = pl.multiple_of(cols[k] * tile, tile)
        acc[rows[k]] += jnp.dot(
            tiles[k], block[pl.ds(start, tile), :], preferred_element_type=jnp.float32
        )
        return carry

    lax.fori_loop(0, count[0], step, 0)
    me = core[0]
    pieces = tile // (own_rows * nrep)
    for t in range(acc.shape[0]):
        for q in range(pieces):
            base = q * nrep * own_rows
            mine = pl.multiple_of(base + me * own_rows, own_rows)
            other = pl.multiple_of(base + (1 - me) * own_rows, own_rows)
            keep[t * pieces + q] = acc[t, pl.ds(mine, own_rows), :]
            send[t * pieces + q] = acc[t, pl.ds(other, own_rows), :].astype(send.dtype)


def add_kernel(core, keep, received, out):
    out[...] = (keep[...] + received[1 - core[0]].astype(jnp.float32)).astype(out.dtype)


def dense_kernel(parts, deg, own, cotangent, w_self, w_neigh, hidden, d_own, send):
    agg = jnp.sum(parts[...].astype(jnp.float32), axis=0)
    degree = deg[...]
    neigh = (agg / degree).astype(jnp.bfloat16)
    feats = own[...]
    pre = jnp.dot(feats, w_self[...], preferred_element_type=jnp.float32)
    pre += jnp.dot(neigh, w_neigh[...], preferred_element_type=jnp.float32)
    square = pre * pre
    t = jnp.tanh(GELU_SCALE * (pre + GELU_CUBE * (pre * square)))
    half = 0.5 * (1.0 + t)
    hidden[...] = (pre * half).astype(hidden.dtype)
    slope = half + 0.5 * pre * (1.0 - t * t) * (GELU_SCALE * (1.0 + 3.0 * GELU_CUBE * square))
    dpre = (cotangent[...].astype(jnp.float32) * slope).astype(jnp.bfloat16)
    across = (((1,), (1,)), ((), ()))
    down = (((0,), (0,)), ((), ()))
    d_own[...] = lax.dot_general(
        dpre, w_self[...], across, preferred_element_type=jnp.float32
    ).astype(d_own.dtype)
    dagg = lax.dot_general(dpre, w_neigh[...], across, preferred_element_type=jnp.float32) / degree
    dagg = dagg.astype(send.dtype)
    grads = [
        lax.dot_general(lhs, dpre, down, preferred_element_type=jnp.float32).astype(send.dtype)
        for lhs in (feats, neigh)
    ]
    n = own.shape[0]
    feat = own.shape[1]
    per = feat // n
    for j in range(send.shape[0]):
        lane, row = divmod(j, 2 * per)
        which, row = divmod(row, per)
        send[j, :n] = dagg
        send[j, n:] = grads[which][row * n : (row + 1) * n, lane * feat : (lane + 1) * feat]


def backward_kernel(rows, cols, count, core, gathered, tiles, keep, send, grad, block, acc):
    nrep, ncol, wide, feat = gathered.shape
    own_rows = wide // 2
    tile = tiles.shape[-1]
    pieces = tile // (own_rows * nrep)
    me = core[0]
    for t in range(block.shape[0]):
        upstream = jnp.concatenate(
            [gathered[c, t * pieces + q, :own_rows] for q in range(pieces) for c in range(nrep)], axis=0
        )
        block[t] = upstream.T
    acc[...] = jnp.zeros_like(acc)

    def step(k, carry):
        part = jnp.dot(block[rows[k]], tiles[k], preferred_element_type=jnp.float32)
        where = cols[k]
        for c in range(nrep):
            acc[where, c] += part[:, c * feat : (c + 1) * feat]
        return carry

    lax.fori_loop(0, count[0], step, 0)
    for t in range(acc.shape[0]):
        keep[t] = acc[t, me].T
        send[t] = acc[t, 1 - me].T.astype(send.dtype)
    share = own_rows // nrep
    start = pl.multiple_of(own_rows + me * share, share)
    total = jnp.sum(gathered[:, :, pl.ds(start, share), :].astype(jnp.float32), axis=(0, 1))
    grad[...] = total.astype(grad.dtype)


def merge_kernel(core, keep, received, grad, out):
    n = keep.shape[1]
    other = 1 - core[0]
    for r in range(keep.shape[0]):
        out[r, :n] = (keep[r] + received[other, r].astype(jnp.float32)).astype(out.dtype)
        out[r, n:] = grad[...]


def finish_kernel(parts, d_src, send):
    n = d_src.shape[0]
    d_src[...] = jnp.sum(parts[:, :n].astype(jnp.float32), axis=0).astype(d_src.dtype)
    share = jnp.sum(parts[:, n:].astype(jnp.float32), axis=0).astype(send.dtype)
    for j in range(send.shape[0]):
        send[j] = share


def weights_kernel(gathered, grad_self, grad_neigh):
    nrep, ncol, share, feat = gathered.shape
    per = feat // (share * nrep)
    for j in range(ncol):
        lane, row = divmod(j, 2 * per)
        which, row = divmod(row, per)
        out = (grad_self, grad_neigh)[which]
        for c in range(nrep):
            start = (row * nrep + c) * share
            out[start : start + share, lane * feat : (lane + 1) * feat] = gathered[c, j].astype(jnp.float32)


def exchange(x, axis):
    return lax.all_to_all(x, axis, split_axis=0, concat_axis=0, tiled=True)


def on_device(
    x_src, x_dst, degree, tile_vals, tile_rows, tile_cols, tile_count, w_self, w_neigh, cotangent
):
    f32, bf16 = jnp.float32, jnp.bfloat16
    nrow, ncol, nrep = lax.axis_size("row"), lax.axis_size("col"), lax.axis_size("rep")
    tiles = tile_vals.reshape(tile_vals.shape[3:])
    rows, cols, count = tile_rows.reshape(-1), tile_cols.reshape(-1), tile_count.reshape(-1)
    core = lax.axis_index("rep").astype(jnp.int32).reshape(1)
    tile = tiles.shape[-1]
    own_src, feat = x_src.shape[1:]
    own_rows = x_dst.shape[1]
    hid = w_self.shape[1]
    row_tiles = own_rows * ncol * nrep // tile
    col_tiles = own_src * nrow * nrep // tile
    shape = jax.ShapeDtypeStruct
    scalars = (rows, cols, count, core)
    cost = pl.CostEstimate(
        flops=2 * tiles.shape[0] * tile * tile * feat, bytes_accessed=tiles.size * 2, transcendentals=0
    )

    source = exchange(jnp.broadcast_to(x_src, (nrow, own_src, feat)), "row")
    source = lax.all_gather(source, "rep", axis=0)
    keep, send = call(
        forward_kernel,
        (shape((ncol, own_rows, feat), f32), shape((ncol, own_rows, feat), bf16)),
        (*scalars, source, tiles),
        in_specs=[SMEM] * 4 + [VMEM] * 2,
        scratch=(
            pltpu.VMEM((own_src * nrow * nrep, feat), bf16),
            pltpu.VMEM((row_tiles, tile, feat), f32),
        ),
        cost=cost,
    )
    received = lax.all_gather(send, "rep", axis=0)
    parts = call(
        add_kernel,
        shape((ncol, own_rows, feat), bf16),
        (core, keep, received),
        in_specs=[SMEM, VMEM, VMEM],
    )
    parts = exchange(parts, "col")
    deg = degree[0].astype(f32)[:, None]
    hidden, d_x_dst, send = call(
        dense_kernel,
        (
            shape((own_rows, hid), bf16),
            shape((own_rows, feat), bf16),
            shape((ncol, 2 * own_rows, feat), bf16),
        ),
        (parts, deg, x_dst[0], cotangent[0], w_self, w_neigh),
    )
    gathered = lax.all_gather(exchange(send, "col"), "rep", axis=0)
    keep, send, grad = call(
        backward_kernel,
        (
            shape((nrow, own_src, feat), f32),
            shape((nrow, own_src, feat), bf16),
            shape((own_rows // nrep, feat), bf16),
        ),
        (*scalars, gathered, tiles),
        in_specs=[SMEM] * 4 + [VMEM] * 2,
        scratch=(
            pltpu.VMEM((row_tiles, feat, tile), bf16),
            pltpu.VMEM((col_tiles, nrep, feat, tile // nrep), f32),
        ),
        cost=cost,
    )
    received = lax.all_gather(send, "rep", axis=0)
    merged = call(
        merge_kernel,
        shape((nrow, own_src + own_rows // nrep, feat), bf16),
        (core, keep, received, grad),
        in_specs=[SMEM] + [VMEM] * 3,
    )
    d_x_src, send = call(
        finish_kernel,
        (shape((own_src, feat), bf16), shape((ncol, own_rows // nrep, feat), bf16)),
        (exchange(merged, "row"),),
    )
    shares = lax.all_gather(exchange(send, "col"), "rep", axis=0)
    grad_self, grad_neigh = call(
        weights_kernel, (shape((feat, hid), f32), shape((feat, hid), f32)), (shares,)
    )
    return (hidden[None], d_x_src[None], d_x_dst[None], grad_self, grad_neigh)


def solution(mesh):
    return jax.shard_map(
        on_device,
        mesh=mesh,
        in_specs=(
            P("col", ("row", "rep"), None),
            P("row", ("col", "rep"), None),
            P("row", ("col", "rep")),
            P("row", "col", "rep", None, None, None),
            P("row", "col", "rep", None),
            P("row", "col", "rep", None),
            P("row", "col", "rep"),
            P(),
            P(),
            P("row", ("col", "rep"), None),
        ),
        out_specs=(
            P("row", ("col", "rep"), None),
            P("col", ("row", "rep"), None),
            P("row", ("col", "rep"), None),
            P(),
            P(),
        ),
        check_vma=False,
    )
```

time: 904 us -> 167 us (0.18)
  waiting for transfers between devices: 736 us -> 32.6 us
  blocking collectives: 118 us -> 74.5 us
  starting transfers between devices: 0.12 us -> 26.7 us
  matrix products: 9.68 us -> 0 us
  loops' own time: 9.25 us -> 0 us
    reduce_scatter x2 -> x0, waiting for transfers between devices: 482 us -> none  [the longest x1 396 us: on_device(): lax.psum_scatter(partial_value, ('col', 'rep'), scatter_dimension=0, tile...]
    psum x1 -> x0, waiting for transfers between devices: 254 us -> none  [on_device(): lax.psum((jnp.dot(own_feats.T, dpre, preferred_element_type=jnp.float32),...]
    all_gather x2 -> x4, blocking collectives: 118 us -> 12.1 us  [the longest x2 4.49 us: on_device(): received = lax.all_gather(send, 'rep', axis=0)]
    all_to_all x0 -> x3, blocking collectives: none -> 62.4 us  [exchange(): return lax.all_to_all(x, axis, split_axis=0, concat_axis=0, tiled=True)]
    all_to_all x0 -> x2, starting transfers between devices: none -> 26.6 us  [exchange(): return lax.all_to_all(x, axis, split_axis=0, concat_axis=0, tiled=True)]
    all_to_all x0 -> x2, waiting for transfers between devices: none -> 19.8 us  [exchange(): return lax.all_to_all(x, axis, split_axis=0, concat_axis=0, tiled=True)]
    all_gather x0 -> x1, waiting for transfers between devices: none -> 12.7 us  [on_device(): gathered = lax.all_gather(exchange(send, 'col'), 'rep', axis=0)]
    dot_general x10 -> x0, matrix products: 9.68 us -> none  [the longest x2 2.27 us: backward_step(): lax.dot_general(matrix, upstream, (((0,), (0,)), ((), ())), preferred_ele...]
where the time goes in v1:
time: 167 us
  blocking collectives  74.5 us (45%)
  waiting for transfers between devices  32.6 us (20%)
  starting transfers between devices  26.7 us (16%)
  between operations  14.7 us (9%)
  local copies, waits for them, and re-layouts  10.3 us (6%)
  Pallas kernels  7.14 us (4%)
    all_to_all x3, blocking collectives, exchange(): return lax.all_to_all(x, axis, split_axis=0, concat_axis=0, tiled=True)  62.4 us
    all_to_all x2, starting transfers between devices, exchange(): return lax.all_to_all(x, axis, split_axis=0, concat_axis=0, tiled=True)  26.6 us
    all_to_all x2, waiting for transfers between devices, exchange(): return lax.all_to_all(x, axis, split_axis=0, concat_axis=0, tiled=True)  19.8 us
    all_gather x1, waiting for transfers between devices, on_device(): gathered = lax.all_gather(exchange(send, 'col'), 'rep', axis=0)  12.7 us
    unnamed x24, local copies, waits for them, and re-layouts  8.1 us
    pallas_call x7, Pallas kernels, call(): pl.pallas_call(kernel, out_shape=out_shape, in_specs=in_specs or [VMEM] *...  7.14 us
    all_gather x2, blocking collectives, on_device(): received = lax.all_gather(send, 'rep', axis=0)  4.49 us
    all_gather x1, blocking collectives, on_device(): source = lax.all_gather(source, 'rep', axis=0)  3.86 us
  transfers between devices with their start and end apart: 3, of which 3 were waited for; matrix products, arithmetic and copies ran while one was open for 1% of the time, Pallas kernels for 0%

profile of v1, /device:TPU:1, one launch (start us, length us, event | category | flops | bytes accessed | tf_op | source)
XLA Modules:
  0.0 166.5 jit_solution(1448403670411772866)
XLA Ops:
  7.2 1.5 broadcast_in_dim.18
  8.7 10.1 %all-to-all-start = ((bf16[8,128,128]{2,1,0:T(8,128)(2,1)}), bf16[8,128,128]{2,1,0:T(8,128)(2,1)S(1)}, u32[]{:S(2)}, u32[]{:S(2)}) async-start(bf16[8,128,128]{2,1,0:T(8,128)(2,1)} %broadcast_in_dim.18), calls=%async_computation | async-start | bytes 524288 | tf_op jit(solution)/shard_map/all_to_all | solution.py:152
  19.4 9.5 %all-to-all-done = bf16[8,128,128]{2,1,0:T(8,128)(2,1)S(1)} async-done(((bf16[8,128,128]{2,1,0:T(8,128)(2,1)}), bf16[8,128,128]{2,1,0:T(8,128)(2,1)S(1)}, u32[]{:S(2)}, u32[]{:S(2)}) %all-to-all-start) | async-done | bytes 262176 | tf_op jit(solution)/shard_map/all_to_all | solution.py:152
  28.9 3.9 %all-gather = bf16[16,128,128]{2,1,0:T(8,128)(2,1)S(1)} all-gather(bf16[8,128,128]{2,1,0:T(8,128)(2,1)S(1)} %all-to-all-done), channel_id=2, replica_groups=mesh['row'=8,'col'=32,'rep'=2] {'rep'}, dimensions={0}, use_global_device_ids=true | all-gather | bytes 786432 | tf_op jit(solution)/shard_map/all_gather | solution.py:176
  32.8 0.0 copy-start
  32.8 1.9 %copy-done = bf16[1,1,1,24,256,256]{5,4,3,2,1,0:T(8,128)(2,1)S(1)} copy-done((bf16[1,1,1,24,256,256]{5,4,3,2,1,0:T(8,128)(2,1)S(1)}, bf16[1,1,1,24,256,256]{5,4,3,2,1,0:T(8,128)(2,1)}, u32[]{:S(2)}) %copy-start) | copy-done | bytes 3145752
  34.7 0.0 copy-start.7
  34.7 0.7 copy-done.7
  35.4 0.0 copy-start.9
  35.4 0.7 copy-done.9
  36.0 0.0 copy-start.11
  36.0 0.0 copy-start.3
  36.0 1.8 %shard_map.137 = (f32[32,32,128]{2,1,0:T(8,128)S(1)}, bf16[32,32,128]{2,1,0:T(8,128)(2,1)S(1)}) custom-call(s32[24]{0:T(128)S(1)} %bitcast.29, s32[24]{0:T(128)S(1)} %bitcast.31, s32[1]{0:T(128)} %bitcast.18.count, s32[1]{0:T(128)} %bitcast.core, bf16[2,8,128,128]{3,2,1,0:T(8,128)(2,1)S(1)} %bitcast.23, bf16[24,256,256]{2,1,0:T(8,128)(2,1)S(1)} %bitcast.20), custom_call_target="tpu_custom_call" | custom-call | flops 402653184 | bytes 3145728 | tf_op jit(solution)/shard_map/pallas_call | solution.py:16
  37.8 0.0 copy-start.1
  37.8 2.3 %all-gather.1 = bf16[64,32,128]{2,1,0:T(8,128)(2,1)S(1)} all-gather(bf16[32,32,128]{2,1,0:T(8,128)(2,1)S(1)} %get-tuple-element.18), channel_id=3, replica_groups=mesh['row'=8,'col'=32,'rep'=2] {'rep'}, dimensions={0}, use_global_device_ids=true | all-gather | bytes 786432 | tf_op jit(solution)/shard_map/all_gather | solution.py:188
  40.1 0.7 shard_map.138
  40.9 16.5 %all-to-all-start.1 = ((bf16[32,32,128]{2,1,0:T(8,128)(2,1)}), bf16[32,32,128]{2,1,0:T(8,128)(2,1)S(1)}, u32[]{:S(2)}, u32[]{:S(2)}) async-start(bf16[32,32,128]{2,1,0:T(8,128)(2,1)} %shard_map.138), calls=%async_computation.1 | async-start | bytes 524288 | tf_op jit(solution)/shard_map/all_to_all | solution.py:152
  57.4 0.0 all-gather.7.cloned.1.call-start
  57.4 0.0 copy-done.11
  57.5 0.5 convert_bitcast_fusion
  58.0 0.7 copy.16.deg
  58.7 10.3 %all-to-all-done.1.parts = bf16[32,32,128]{2,1,0:T(8,128)(2,1)S(1)} async-done(((bf16[32,32,128]{2,1,0:T(8,128)(2,1)}), bf16[32,32,128]{2,1,0:T(8,128)(2,1)S(1)}, u32[]{:S(2)}, u32[]{:S(2)}) %all-to-all-start.1) | async-done | bytes 262176 | tf_op jit(solution)/shard_map/all_to_all | solution.py:152
  69.0 0.0 copy-done.3
  69.0 0.0 copy-start.4
  69.0 0.9 copy-done.4
  69.9 0.0 copy-start.5
  69.9 0.8 copy-done.5
  70.7 0.0 copy-start.6
  70.7 0.7 copy-done.6
  71.4 1.0 shard_map.139
  72.4 19.6 %all_to_all.25 = bf16[32,64,128]{2,1,0:T(8,128)(2,1)} all-to-all(bf16[32,64,128]{2,1,0:T(8,128)(2,1)S(1)} %get-tuple-element.20), channel_id=1, replica_groups=mesh['row'=8,'col'=32,'rep'=2] {'col'}, dimensions={0} | all-to-all | bytes 1048576 | tf_op jit(solution)/shard_map/all_to_all | solution.py:152
  92.0 0.0 all-gather.7.cloned.1.call-update
  92.1 12.7 %all-gather.7.cloned.1.call-done = bf16[64,64,128]{2,1,0:T(8,128)(2,1)} async-done(((bf16[32,64,128]{2,1,0:T(8,128)(2,1)}), bf16[64,64,128]{2,1,0:T(8,128)(2,1)}) %all-gather.7.cloned.1.call-update) | async-done | bytes 1048592 | tf_op jit(solution)/shard_map/all_gather | solution.py:206
  104.8 0.0 copy-done.1
  104.8 0.0 copy-start.2
  104.8 1.2 copy-done.2
  106.0 0.0 copy-start.8
  106.0 0.7 copy-done.8
  106.7 0.0 copy-start.10
  106.7 0.7 copy-done.10
  107.3 2.0 %shard_map.140 = (f32[8,128,128]{2,1,0:T(8,128)S(1)}, bf16[8,128,128]{2,1,0:T(8,128)(2,1)S(1)}, bf16[16,128]{1,0:T(8,128)(2,1)S(1)}) custom-call(s32[24]{0:T(128)S(1)} %bitcast.30, s32[24]{0:T(128)S(1)} %bitcast.32, s32[1]{0:T(128)} %bitcast.19.count, s32[1]{0:T(128)} %bitcast.core, bf16[2,32,64,128]{3,2,1,0:T(8,128)(2,1)S(1)} %bitcast.26, ...), custom_call_target="tpu_custom_call" | custom-call | flops 402653184 | bytes 3145728 | tf_op jit(solution)/shard_map/pallas_call | solution.py:16
  109.4 2.2 %all-gather.3 = bf16[16,128,128]{2,1,0:T(8,128)(2,1)S(1)} all-gather(bf16[8,128,128]{2,1,0:T(8,128)(2,1)S(1)} %get-tuple-element.22), channel_id=5, replica_groups=mesh['row'=8,'col'=32,'rep'=2] {'rep'}, dimensions={0}, use_global_device_ids=true | all-gather | bytes 786432 | tf_op jit(solution)/shard_map/all_gather | solution.py:222
  111.5 0.1 shard_map.141
  111.6 18.8 %all_to_all.26.parts = bf16[8,144,128]{2,1,0:T(8,128)(2,1)S(1)} all-to-all(bf16[8,144,128]{2,1,0:T(8,128)(2,1)S(1)} %shard_map.141), channel_id=1, replica_groups=mesh['row'=8,'col'=32,'rep'=2] {'row'}, dimensions={0} | all-to-all | bytes 589824 | tf_op jit(solution)/shard_map/all_to_all | solution.py:152
  130.4 0.7 shard_map.142
  131.1 24.0 %all_to_all.27 = bf16[32,16,128]{2,1,0:T(8,128)(2,1)S(1)} all-to-all(bf16[32,16,128]{2,1,0:T(8,128)(2,1)S(1)} %get-tuple-element.26), channel_id=1, replica_groups=mesh['row'=8,'col'=32,'rep'=2] {'col'}, dimensions={0} | all-to-all | bytes 262144 | tf_op jit(solution)/shard_map/all_to_all | solution.py:152
  155.1 3.8 %all-gather.4 = bf16[64,16,128]{2,1,0:T(8,128)(2,1)S(1)} all-gather(bf16[32,16,128]{2,1,0:T(8,128)(2,1)S(1)} %all_to_all.27), channel_id=6, replica_groups=mesh['row'=8,'col'=32,'rep'=2] {'rep'}, dimensions={0}, use_global_device_ids=true | all-gather | bytes 393216 | tf_op jit(solution)/shard_map/all_gather | solution.py:234
  158.8 0.8 shard_map.143
Async XLA Ops:
  8.7 20.3 %all-to-all-start = ((bf16[8,128,128]{2,1,0:T(8,128)(2,1)}), bf16[8,128,128]{2,1,0:T(8,128)(2,1)S(1)}, u32[]{:S(2)}, u32[]{:S(2)}) async-start(bf16[8,128,128]{2,1,0:T(8,128)(2,1)} %broadcast_in_dim.18), calls=%async_computation | async-start | bytes 524288 | tf_op jit(solution)/shard_map/all_to_all | solution.py:152
  32.8 1.9 %copy-start = (bf16[1,1,1,24,256,256]{5,4,3,2,1,0:T(8,128)(2,1)S(1)}, bf16[1,1,1,24,256,256]{5,4,3,2,1,0:T(8,128)(2,1)}, u32[]{:S(2)}) copy-start(bf16[1,1,1,24,256,256]{5,4,3,2,1,0:T(8,128)(2,1)} %param.13) | copy-start | bytes 9437188
  34.7 0.7 copy-start.7
  35.4 0.7 copy-start.9
  36.0 21.4 %copy-start.11 = (s32[1,32]{1,0:T(1,128)S(1)}, s32[1,32]{1,0:T(1,128)}, u32[]{:S(2)}) copy-start(s32[1,32]{1,0:T(1,128)} %param.12) | copy-start | bytes 388
  36.0 33.0 %copy-start.3 = (bf16[128,512]{1,0:T(8,128)(2,1)S(1)}, bf16[128,512]{1,0:T(8,128)(2,1)}, u32[]{:S(2)}) copy-start(bf16[128,512]{1,0:T(8,128)(2,1)} %w_self.1) | copy-start | bytes 393220
  37.8 67.0 %copy-start.1 = (bf16[1,1,1,24,256,256]{5,4,3,2,1,0:T(8,128)(2,1)S(1)}, bf16[1,1,1,24,256,256]{5,4,3,2,1,0:T(8,128)(2,1)}, u32[]{:S(2)}) copy-start(bf16[1,1,1,24,256,256]{5,4,3,2,1,0:T(8,128)(2,1)} %param.13) | copy-start | bytes 9437188
  40.9 28.2 %all-to-all-start.1 = ((bf16[32,32,128]{2,1,0:T(8,128)(2,1)}), bf16[32,32,128]{2,1,0:T(8,128)(2,1)S(1)}, u32[]{:S(2)}, u32[]{:S(2)}) async-start(bf16[32,32,128]{2,1,0:T(8,128)(2,1)} %shard_map.138), calls=%async_computation.1 | async-start | bytes 524288 | tf_op jit(solution)/shard_map/all_to_all | solution.py:152
  57.4 47.4 %all-gather.7.cloned.1.call-start = ((), (), s32[]{:S(2)}) async-start(), calls=%async_computation.5 | async-start | bytes 1572864 | tf_op jit(solution)/shard_map/all_gather | solution.py:206
  69.0 0.9 copy-start.4
  69.9 0.8 copy-start.5
  70.7 0.7 copy-start.6
  104.8 1.2 copy-start.2
  106.0 0.7 copy-start.8
  106.7 0.7 copy-start.10
Sparse Core Ops, SparseCore 0:
  92.2 12.5 all-gather.6

commit v2 on v1

--- a/solution.py
+++ b/solution.py
@@ -10,38 +10,71 @@
 MIB = 1 << 20
 VMEM = pl.BlockSpec(memory_space=pltpu.VMEM)
 SMEM = pl.BlockSpec(memory_space=pltpu.SMEM)
-
-
-def call(kernel, out_shape, operands, in_specs=None, scratch=(), limit=16, cost=None):
+ANY = pl.BlockSpec(memory_space=pl.ANY)
+
+
+def call(kernel, out_shape, operands, in_specs=None, out_specs=None, scratch=(), limit=16, cost=None):
     return pl.pallas_call(
         kernel,
         out_shape=out_shape,
         in_specs=in_specs or [VMEM] * len(operands),
-        out_specs=jax.tree.map(lambda _: VMEM, out_shape),
+        out_specs=out_specs or jax.tree.map(lambda _: VMEM, out_shape),
         scratch_shapes=list(scratch),
         compiler_params=pltpu.CompilerParams(vmem_limit_bytes=limit * MIB),
         cost_estimate=cost,
     )(*operands)
 
 
-def forward_kernel(rows, cols, count, core, source, tiles, keep, send, block, acc):
+def each_live(count, step, group=8):
+    def many(g, carry):
+        for u in range(group):
+            step(g * group + u)
+        return carry
+
+    def one(k, carry):
+        step(k)
+        return carry
+
+    groups = count // group
+    lax.fori_loop(0, groups, many, 0)
+    lax.fori_loop(groups * group, count, one, 0)
+
+
+def spread_kernel(x, out, sems):
+    copies = [pltpu.make_async_copy(x.at[0], out.at[r], sems.at[r]) for r in range(out.shape[0])]
+    for copy in copies:
+        copy.start()
+    for copy in copies:
+        copy.wait()
+
+
+def fetch_kernel(*refs):
+    n = len(refs) // 2
+    sems = refs[2 * n]
+    copies = [pltpu.make_async_copy(refs[i], refs[n + i], sems.at[i]) for i in range(n)]
+    for copy in copies:
+        copy.start()
+    for copy in copies:
+        copy.wait()
+
+
+def forward_kernel(meta, source, tiles, keep, send, block, acc):
     nrep, nrow, part, _ = source.shape
-    tile = tiles.shape[-1]
+    slots, tile = tiles.shape[0], tiles.shape[-1]
     own_rows = keep.shape[1]
     for r in range(nrow):
         for c in range(nrep):
             block[pl.ds((r * nrep + c) * part, part), :] = source[c, r]
     acc[...] = jnp.zeros_like(acc)
 
-    def step(k, carry):
-        start = pl.multiple_of(cols[k] * tile, tile)
-        acc[rows[k]] += jnp.dot(
+    def step(k):
+        start = pl.multiple_of(meta[slots + k] * tile, tile)
+        acc[meta[k]] += jnp.dot(
             tiles[k], block[pl.ds(start, tile), :], preferred_element_type=jnp.float32
         )
-        return carry
-
-    lax.fori_loop(0, count[0], step, 0)
-    me = core[0]
+
+    each_live(meta[2 * slots], step)
+    me = meta[2 * slots + 1]
     pieces = tile // (own_rows * nrep)
     for t in range(acc.shape[0]):
         for q in range(pieces):
@@ -52,13 +85,17 @@
             send[t * pieces + q] = acc[t, pl.ds(other, own_rows), :].astype(send.dtype)
 
 
-def add_kernel(core, keep, received, out):
-    out[...] = (keep[...] + received[1 - core[0]].astype(jnp.float32)).astype(out.dtype)
+def add_kernel(meta, keep, received, out):
+    other = 1 - meta[meta.shape[0] - 1]
+    out[...] = (keep[...] + received[other].astype(jnp.float32)).astype(out.dtype)
 
 
 def dense_kernel(parts, deg, own, cotangent, w_self, w_neigh, hidden, d_own, send):
     agg = jnp.sum(parts[...].astype(jnp.float32), axis=0)
-    degree = deg[...]
+    n = own.shape[0]
+    along = jnp.broadcast_to(deg[...].astype(jnp.float32), (n, n))
+    diagonal = lax.broadcasted_iota(jnp.int32, (n, n), 0) == lax.broadcasted_iota(jnp.int32, (n, n), 1)
+    degree = jnp.sum(jnp.where(diagonal, along, 0.0), axis=1, keepdims=True)
     neigh = (agg / degree).astype(jnp.bfloat16)
     feats = own[...]
     pre = jnp.dot(feats, w_self[...], preferred_element_type=jnp.float32)
@@ -80,7 +117,6 @@
         lax.dot_general(lhs, dpre, down, preferred_element_type=jnp.float32).astype(send.dtype)
         for lhs in (feats, neigh)
     ]
-    n = own.shape[0]
     feat = own.shape[1]
     per = feat // n
     for j in range(send.shape[0]):
@@ -90,42 +126,50 @@
         send[j, n:] = grads[which][row * n : (row + 1) * n, lane * feat : (lane + 1) * feat]
 
 
-def backward_kernel(rows, cols, count, core, gathered, tiles, keep, send, grad, block, acc):
-    nrep, ncol, wide, feat = gathered.shape
-    own_rows = wide // 2
-    tile = tiles.shape[-1]
+def split_kernel(both, dagg, share):
+    n = dagg.shape[1]
+    dagg[...] = both[:, :n]
+    share[...] = jnp.sum(both[:, n:].astype(jnp.float32), axis=0)
+
+
+def backward_kernel(meta, gathered, tiles, share, keep, send, block, acc):
+    nrep, ncol, own_rows, feat = gathered.shape
+    slots, tile = tiles.shape[0], tiles.shape[-1]
     pieces = tile // (own_rows * nrep)
-    me = core[0]
+    me = meta[2 * slots + 1]
     for t in range(block.shape[0]):
         upstream = jnp.concatenate(
-            [gathered[c, t * pieces + q, :own_rows] for q in range(pieces) for c in range(nrep)], axis=0
+            [gathered[c, t * pieces + q] for q in range(pieces) for c in range(nrep)], axis=0
         )
         block[t] = upstream.T
     acc[...] = jnp.zeros_like(acc)
 
-    def step(k, carry):
-        part = jnp.dot(block[rows[k]], tiles[k], preferred_element_type=jnp.float32)
-        where = cols[k]
+    def step(k):
+        part = jnp.dot(block[meta[k]], tiles[k], preferred_element_type=jnp.float32)
+        where = meta[slots + k]
         for c in range(nrep):
             acc[where, c] += part[:, c * feat : (c + 1) * feat]
-        return carry
-
-    lax.fori_loop(0, count[0], step, 0)
+
+    each_live(meta[2 * slots], step)
+    n = keep.shape[1]
     for t in range(acc.shape[0]):
         keep[t] = acc[t, me].T
-        send[t] = acc[t, 1 - me].T.astype(send.dtype)
-    share = own_rows // nrep
-    start = pl.multiple_of(own_rows + me * share, share)
-    total = jnp.sum(gathered[:, :, pl.ds(start, share), :].astype(jnp.float32), axis=(0, 1))
-    grad[...] = total.astype(grad.dtype)
-
-
-def merge_kernel(core, keep, received, grad, out):
-    n = keep.shape[1]
-    other = 1 - core[0]
-    for r in range(keep.shape[0]):
-        out[r, :n] = (keep[r] + received[other, r].astype(jnp.float32)).astype(out.dtype)
-        out[r, n:] = grad[...]
+        send[t * n : (t + 1) * n] = acc[t, 1 - me].T.astype(send.dtype)
+    half = own_rows // nrep
+    start = pl.multiple_of((1 - me) * half, half)
+    send[acc.shape[0] * n :] = share[pl.ds(start, half), :].astype(send.dtype)
+
+
+def merge_kernel(meta, keep, received, share, out):
+    me = meta[meta.shape[0] - 1]
+    nrow, n, _ = keep.shape
+    half = out.shape[1] - n
+    start = pl.multiple_of(me * half, half)
+    grad = share[pl.ds(start, half), :] + received[1 - me, nrow * n :].astype(jnp.float32)
+    for r in range(nrow):
+        part = received[1 - me, r * n : (r + 1) * n].astype(jnp.float32)
+        out[r, :n] = (keep[r] + part).astype(out.dtype)
+        out[r, n:] = grad.astype(out.dtype)
 
 
 def finish_kernel(parts, d_src, send):
@@ -158,27 +202,50 @@
     f32, bf16 = jnp.float32, jnp.bfloat16
     nrow, ncol, nrep = lax.axis_size("row"), lax.axis_size("col"), lax.axis_size("rep")
     tiles = tile_vals.reshape(tile_vals.shape[3:])
-    rows, cols, count = tile_rows.reshape(-1), tile_cols.reshape(-1), tile_count.reshape(-1)
-    core = lax.axis_index("rep").astype(jnp.int32).reshape(1)
-    tile = tiles.shape[-1]
+    meta = jnp.concatenate(
+        [
+            tile_rows.reshape(-1),
+            tile_cols.reshape(-1),
+            tile_count.reshape(-1),
+            lax.axis_index("rep").astype(jnp.int32).reshape(1),
+        ]
+    )
+    slots, tile = tiles.shape[:2]
     own_src, feat = x_src.shape[1:]
     own_rows = x_dst.shape[1]
+    half = own_rows // nrep
     hid = w_self.shape[1]
     row_tiles = own_rows * ncol * nrep // tile
     col_tiles = own_src * nrow * nrep // tile
     shape = jax.ShapeDtypeStruct
-    scalars = (rows, cols, count, core)
     cost = pl.CostEstimate(
-        flops=2 * tiles.shape[0] * tile * tile * feat, bytes_accessed=tiles.size * 2, transcendentals=0
-    )
-
-    source = exchange(jnp.broadcast_to(x_src, (nrow, own_src, feat)), "row")
+        flops=2 * slots * tile * tile * feat, bytes_accessed=tiles.size * 2, transcendentals=0
+    )
+
+    source = call(
+        spread_kernel,
+        shape((nrow, own_src, feat), bf16),
+        (x_src,),
+        in_specs=[ANY],
+        out_specs=ANY,
+        scratch=(pltpu.SemaphoreType.DMA((nrow,)),),
+    )
+    source = exchange(source, "row")
+    held = (tiles, degree, x_dst[0], cotangent[0], w_self, w_neigh)
+    tiles, *held = call(
+        fetch_kernel,
+        tuple(shape(x.shape, x.dtype) for x in held),
+        held,
+        in_specs=[ANY] * len(held),
+        scratch=(pltpu.SemaphoreType.DMA((len(held),)),),
+        cost=pl.CostEstimate(flops=0, bytes_accessed=tiles.size * 4, transcendentals=0),
+    )
     source = lax.all_gather(source, "rep", axis=0)
     keep, send = call(
         forward_kernel,
         (shape((ncol, own_rows, feat), f32), shape((ncol, own_rows, feat), bf16)),
-        (*scalars, source, tiles),
-        in_specs=[SMEM] * 4 + [VMEM] * 2,
+        (meta, source, tiles),
+        in_specs=[SMEM, VMEM, VMEM],
         scratch=(
             pltpu.VMEM((own_src * nrow * nrep, feat), bf16),
             pltpu.VMEM((row_tiles, tile, feat), f32),
@@ -189,11 +256,10 @@
     parts = call(
         add_kernel,
         shape((ncol, own_rows, feat), bf16),
-        (core, keep, received),
+        (meta, keep, received),
         in_specs=[SMEM, VMEM, VMEM],
     )
     parts = exchange(parts, "col")
-    deg = degree[0].astype(f32)[:, None]
     hidden, d_x_dst, send = call(
         dense_kernel,
         (
@@ -201,18 +267,19 @@
             shape((own_rows, feat), bf16),
             shape((ncol, 2 * own_rows, feat), bf16),
         ),
-        (parts, deg, x_dst[0], cotangent[0], w_self, w_neigh),
-    )
-    gathered = lax.all_gather(exchange(send, "col"), "rep", axis=0)
-    keep, send, grad = call(
+        (parts, *held),
+    )
+    dagg, share = call(
+        split_kernel,
+        (shape((ncol, own_rows, feat), bf16), shape((own_rows, feat), f32)),
+        (exchange(send, "col"),),
+    )
+    gathered = lax.all_gather(dagg, "rep", axis=0)
+    keep, send = call(
         backward_kernel,
-        (
-            shape((nrow, own_src, feat), f32),
-            shape((nrow, own_src, feat), bf16),
-            shape((own_rows // nrep, feat), bf16),
-        ),
-        (*scalars, gathered, tiles),
-        in_specs=[SMEM] * 4 + [VMEM] * 2,
+        (shape((nrow, own_src, feat), f32), shape((nrow * own_src + half, feat), bf16)),
+        (meta, gathered, tiles, share),
+        in_specs=[SMEM] + [VMEM] * 3,
         scratch=(
             pltpu.VMEM((row_tiles, feat, tile), bf16),
             pltpu.VMEM((col_tiles, nrep, feat, tile // nrep), f32),
@@ -222,13 +289,13 @@
     received = lax.all_gather(send, "rep", axis=0)
     merged = call(
         merge_kernel,
-        shape((nrow, own_src + own_rows // nrep, feat), bf16),
-        (core, keep, received, grad),
+        shape((nrow, own_src + half, feat), bf16),
+        (meta, keep, received, share),
         in_specs=[SMEM] + [VMEM] * 3,
     )
     d_x_src, send = call(
         finish_kernel,
-        (shape((own_src, feat), bf16), shape((ncol, own_rows // nrep, feat), bf16)),
+        (shape((own_src, feat), bf16), shape((ncol, half, feat), bf16)),
         (exchange(merged, "row"),),
     )
     shares = lax.all_gather(exchange(send, "col"), "rep", axis=0)

time: 167 us -> 124 us (0.74)
  waiting for transfers between devices: 32.6 us -> 3.05 us
  blocking collectives: 74.5 us -> 93.8 us
  starting transfers between devices: 26.7 us -> 10.1 us
  between operations: 14.7 us -> 1.38 us
  local copies, waits for them, and re-layouts: 10.3 us -> 6.56 us
    all_to_all x2 -> x1, waiting for transfers between devices: 19.8 us -> 3.05 us  [exchange(): return lax.all_to_all(x, axis, split_axis=0, concat_axis=0, tiled=True)]
    all_to_all x2 -> x1, starting transfers between devices: 26.6 us -> 10.1 us  [exchange(): return lax.all_to_all(x, axis, split_axis=0, concat_axis=0, tiled=True)]
    all_to_all x3 -> x4, blocking collectives: 62.4 us -> 75.8 us  [exchange(): return lax.all_to_all(x, axis, split_axis=0, concat_axis=0, tiled=True)]
    all_gather x1 -> x0, waiting for transfers between devices: 12.7 us -> none  [on_device(): gathered = lax.all_gather(exchange(send, 'col'), 'rep', axis=0)]
    all_gather x0 -> x1, blocking collectives: none -> 5.09 us  [on_device(): gathered = lax.all_gather(dagg, 'rep', axis=0)]
    unnamed x24 -> x18, local copies, waits for them, and re-layouts: 8.1 us -> 6.56 us
    pallas_call x7 -> x10, Pallas kernels: 7.14 us -> 7.97 us  [call(): pl.pallas_call(kernel, out_shape=out_shape, in_specs=in_specs or [VMEM] *...]
  transfers between devices with their start and end apart: 3 -> 1, of which waited for: 3 -> 1; matrix products, arithmetic and copies ran while one was open for 1% -> 0% of each run, Pallas kernels for 0% -> 1%
where the time goes in v2:
time: 124 us; the launch traced here: 123 us
  blocking collectives  93.8 us (76%)
  starting transfers between devices  10.1 us (8%)
  Pallas kernels  7.97 us (6%)
  local copies, waits for them, and re-layouts  6.56 us (5%)
  waiting for transfers between devices  3.05 us (2%)
  between operations  1.38 us (1%)
    all_to_all x4, blocking collectives, exchange(): return lax.all_to_all(x, axis, split_axis=0, concat_axis=0, tiled=True)  75.8 us
    all_to_all x1, starting transfers between devices, exchange(): return lax.all_to_all(x, axis, split_axis=0, concat_axis=0, tiled=True)  10.1 us
    pallas_call x10, Pallas kernels, call(): pl.pallas_call(kernel, out_shape=out_shape, in_specs=in_specs or [VMEM] *...  7.97 us
    unnamed x18, local copies, waits for them, and re-layouts  6.56 us
    all_gather x1, blocking collectives, on_device(): gathered = lax.all_gather(dagg, 'rep', axis=0)  5.09 us
    all_gather x1, blocking collectives, on_device(): shares = lax.all_gather(exchange(send, 'col'), 'rep', axis=0)  4.49 us
    all_gather x2, blocking collectives, on_device(): received = lax.all_gather(send, 'rep', axis=0)  4.37 us
    all_gather x1, blocking collectives, on_device(): source = lax.all_gather(source, 'rep', axis=0)  4.07 us
  transfers between devices with their start and end apart: 1, of which 1 were waited for; matrix products, arithmetic and copies ran while one was open for 0% of the time, Pallas kernels for 1%

profile of v2, /device:TPU:1, one launch (start us, length us, event | category | flops | bytes accessed | tf_op | source)
XLA Modules:
  0.0 123.0 jit_solution(5572488485218042201)
XLA Ops:
  0.6 0.0 copy-start.4
  0.6 0.7 copy-done.4
  1.4 0.0 copy-start.7
  1.4 0.0 copy-start.8
  1.4 0.8 shard_map.137
  2.2 10.1 %all-to-all-start = ((bf16[8,128,128]{2,1,0:T(8,128)(2,1)}), bf16[8,128,128]{2,1,0:T(8,128)(2,1)}, u32[]{:S(2)}, u32[]{:S(2)}) async-start(bf16[8,128,128]{2,1,0:T(8,128)(2,1)} %shard_map.137), calls=%async_computation | async-start | bytes 524288 | tf_op jit(solution)/shard_map/all_to_all | solution.py:196
  12.9 0.0 copy-start
  12.9 1.9 %copy-done = bf16[1,1,1,24,256,256]{5,4,3,2,1,0:T(8,128)(2,1)S(1)} copy-done((bf16[1,1,1,24,256,256]{5,4,3,2,1,0:T(8,128)(2,1)S(1)}, bf16[1,1,1,24,256,256]{5,4,3,2,1,0:T(8,128)(2,1)}, u32[]{:S(2)}) %copy-start) | copy-done | bytes 3145752
  14.8 0.0 copy-start.1
  14.8 0.9 copy-done.1
  15.7 0.0 copy-start.2
  15.7 0.9 copy-done.2
  16.6 0.0 copy-start.3
  16.6 0.8 copy-done.3
  17.4 0.0 copy-start.5
  17.4 0.7 copy-done.5
  18.1 0.0 copy-start.6
  18.1 0.7 copy-done.6
  18.7 0.7 shard_map.138
  19.4 0.0 copy-done.7
  19.4 0.0 copy-done.8
  19.4 0.1 pad_add_fusion.meta
  19.5 3.1 %all-to-all-done = bf16[8,128,128]{2,1,0:T(8,128)(2,1)} async-done(((bf16[8,128,128]{2,1,0:T(8,128)(2,1)}), bf16[8,128,128]{2,1,0:T(8,128)(2,1)}, u32[]{:S(2)}, u32[]{:S(2)}) %all-to-all-start) | async-done | bytes 262176 | tf_op jit(solution)/shard_map/all_to_all | solution.py:196
  22.6 4.1 %all-gather = bf16[16,128,128]{2,1,0:T(8,128)(2,1)S(1)} all-gather(bf16[8,128,128]{2,1,0:T(8,128)(2,1)} %all-to-all-done), channel_id=2, replica_groups=mesh['row'=8,'col'=32,'rep'=2] {'rep'}, dimensions={0}, use_global_device_ids=true | all-gather | bytes 786432 | tf_op jit(solution)/shard_map/all_gather | solution.py:243
  26.6 1.2 %shard_map.139 = (f32[32,32,128]{2,1,0:T(8,128)S(1)}, bf16[32,32,128]{2,1,0:T(8,128)(2,1)S(1)}) custom-call(s32[50]{0:T(128)S(1)} %pad_add_fusion.meta, bf16[2,8,128,128]{3,2,1,0:T(8,128)(2,1)S(1)} %bitcast.20, bf16[24,256,256]{2,1,0:T(8,128)(2,1)S(1)} %get-tuple-element.24.tiles), custom_call_target="tpu_custom_call" | custom-call | flops 402653184 | bytes 3145728 | tf_op jit(solution)/shard_map/pallas_call | solution.py:17
  27.9 2.2 %all-gather.1 = bf16[64,32,128]{2,1,0:T(8,128)(2,1)S(1)} all-gather(bf16[32,32,128]{2,1,0:T(8,128)(2,1)S(1)} %get-tuple-element.26), channel_id=3, replica_groups=mesh['row'=8,'col'=32,'rep'=2] {'rep'}, dimensions={0}, use_global_device_ids=true | all-gather | bytes 786432 | tf_op jit(solution)/shard_map/all_gather | solution.py:255
  30.1 0.6 shard_map.140
  30.7 25.2 %all_to_all.25.parts = bf16[32,32,128]{2,1,0:T(8,128)(2,1)S(1)} all-to-all(bf16[32,32,128]{2,1,0:T(8,128)(2,1)S(1)} %shard_map.140), channel_id=1, replica_groups=mesh['row'=8,'col'=32,'rep'=2] {'col'}, dimensions={0} | all-to-all | bytes 524288 | tf_op jit(solution)/shard_map/all_to_all | solution.py:196
  55.9 1.1 shard_map.141
  56.9 19.5 %all_to_all.26.both = bf16[32,64,128]{2,1,0:T(8,128)(2,1)S(1)} all-to-all(bf16[32,64,128]{2,1,0:T(8,128)(2,1)S(1)} %get-tuple-element.33), channel_id=1, replica_groups=mesh['row'=8,'col'=32,'rep'=2] {'col'}, dimensions={0} | all-to-all | bytes 1048576 | tf_op jit(solution)/shard_map/all_to_all | solution.py:196
  76.4 0.1 shard_map.142
  76.5 5.1 %all-gather.2 = bf16[64,32,128]{2,1,0:T(8,128)(2,1)S(1)} all-gather(bf16[32,32,128]{2,1,0:T(8,128)(2,1)S(1)} %get-tuple-element.34), channel_id=4, replica_groups=mesh['row'=8,'col'=32,'rep'=2] {'rep'}, dimensions={0}, use_global_device_ids=true | all-gather | bytes 786432 | tf_op jit(solution)/shard_map/all_gather | solution.py:277
  81.6 1.5 %shard_map.143 = (f32[8,128,128]{2,1,0:T(8,128)S(1)}, bf16[1040,128]{1,0:T(8,128)(2,1)S(1)}) custom-call(s32[50]{0:T(128)S(1)} %pad_add_fusion.meta, bf16[2,32,32,128]{3,2,1,0:T(8,128)(2,1)S(1)} %bitcast.19, bf16[24,256,256]{2,1,0:T(8,128)(2,1)S(1)} %get-tuple-element.24.tiles, f32[32,128]{1,0:T(8,128)S(1)} %get-tuple-element.35.share), custom_call_target="tpu_custom_call" | custom-call | flops 402653184 | bytes 3145728 | tf_op jit(solution)/shard_map/pallas_call | solution.py:17
  83.1 2.2 %all-gather.3 = bf16[2080,128]{1,0:T(8,128)(2,1)S(1)} all-gather(bf16[1040,128]{1,0:T(8,128)(2,1)S(1)} %get-tuple-element.37), channel_id=5, replica_groups=mesh['row'=8,'col'=32,'rep'=2] {'rep'}, dimensions={0}, use_global_device_ids=true | all-gather | bytes 798720 | tf_op jit(solution)/shard_map/all_gather | solution.py:289
  85.3 0.6 shard_map.144
  85.9 13.9 %all_to_all.27.parts = bf16[8,144,128]{2,1,0:T(8,128)(2,1)S(1)} all-to-all(bf16[8,144,128]{2,1,0:T(8,128)(2,1)S(1)} %shard_map.144), channel_id=1, replica_groups=mesh['row'=8,'col'=32,'rep'=2] {'row'}, dimensions={0} | all-to-all | bytes 589824 | tf_op jit(solution)/shard_map/all_to_all | solution.py:196
  99.8 0.7 shard_map.145
  100.5 17.2 %all_to_all.28 = bf16[32,16,128]{2,1,0:T(8,128)(2,1)S(1)} all-to-all(bf16[32,16,128]{2,1,0:T(8,128)(2,1)S(1)} %get-tuple-element.40), channel_id=1, replica_groups=mesh['row'=8,'col'=32,'rep'=2] {'col'}, dimensions={0} | all-to-all | bytes 262144 | tf_op jit(solution)/shard_map/all_to_all | solution.py:196
  117.7 4.5 %all-gather.4 = bf16[64,16,128]{2,1,0:T(8,128)(2,1)S(1)} all-gather(bf16[32,16,128]{2,1,0:T(8,128)(2,1)S(1)} %all_to_all.28), channel_id=6, replica_groups=mesh['row'=8,'col'=32,'rep'=2] {'rep'}, dimensions={0}, use_global_device_ids=true | all-gather | bytes 393216 | tf_op jit(solution)/shard_map/all_gather | solution.py:301
  122.1 0.8 shard_map.146
Async XLA Ops:
  0.6 0.8 copy-start.4
  1.4 18.0 %copy-start.7 = (s32[1,1,1,24]{3,2,1,0:T(1,128)S(1)}, s32[1,1,1,24]{3,2,1,0:T(1,128)}, u32[]{:S(2)}) copy-start(s32[1,1,1,24]{3,2,1,0:T(1,128)} %param.15) | copy-start | bytes 292
  1.4 18.0 %copy-start.8 = (s32[1,1,1,24]{3,2,1,0:T(1,128)S(1)}, s32[1,1,1,24]{3,2,1,0:T(1,128)}, u32[]{:S(2)}) copy-start(s32[1,1,1,24]{3,2,1,0:T(1,128)} %param.14) | copy-start | bytes 292
  2.2 20.4 %all-to-all-start = ((bf16[8,128,128]{2,1,0:T(8,128)(2,1)}), bf16[8,128,128]{2,1,0:T(8,128)(2,1)}, u32[]{:S(2)}, u32[]{:S(2)}) async-start(bf16[8,128,128]{2,1,0:T(8,128)(2,1)} %shard_map.137), calls=%async_computation | async-start | bytes 524288 | tf_op jit(solution)/shard_map/all_to_all | solution.py:196
  12.9 1.9 %copy-start = (bf16[1,1,1,24,256,256]{5,4,3,2,1,0:T(8,128)(2,1)S(1)}, bf16[1,1,1,24,256,256]{5,4,3,2,1,0:T(8,128)(2,1)}, u32[]{:S(2)}) copy-start(bf16[1,1,1,24,256,256]{5,4,3,2,1,0:T(8,128)(2,1)} %param.13) | copy-start | bytes 9437188
  14.8 0.9 copy-start.1
  15.7 0.9 copy-start.2
  16.6 0.8 copy-start.3
  17.4 0.7 copy-start.5
  18.1 0.7 copy-start.6

commit v3 on v2

--- a/solution.py
+++ b/solution.py
@@ -40,12 +40,9 @@
     lax.fori_loop(groups * group, count, one, 0)
 
 
-def spread_kernel(x, out, sems):
-    copies = [pltpu.make_async_copy(x.at[0], out.at[r], sems.at[r]) for r in range(out.shape[0])]
-    for copy in copies:
-        copy.start()
-    for copy in copies:
-        copy.wait()
+def spread_kernel(x, out):
+    for r in range(out.shape[0]):
+        out[r] = x[0]
 
 
 def fetch_kernel(*refs):
@@ -58,7 +55,9 @@
         copy.wait()
 
 
-def forward_kernel(meta, source, tiles, keep, send, block, acc):
+def forward_kernel(scalars, source, tiles, keep, send, block, acc, meta, sem):
+    copy = pltpu.make_async_copy(scalars, meta, sem)
+    copy.start()
     nrep, nrow, part, _ = source.shape
     slots, tile = tiles.shape[0], tiles.shape[-1]
     own_rows = keep.shape[1]
@@ -66,6 +65,7 @@
         for c in range(nrep):
             block[pl.ds((r * nrep + c) * part, part), :] = source[c, r]
     acc[...] = jnp.zeros_like(acc)
+    copy.wait()
 
     def step(k):
         start = pl.multiple_of(meta[slots + k] * tile, tile)
@@ -85,8 +85,8 @@
             send[t * pieces + q] = acc[t, pl.ds(other, own_rows), :].astype(send.dtype)
 
 
-def add_kernel(meta, keep, received, out):
-    other = 1 - meta[meta.shape[0] - 1]
+def add_kernel(core, keep, received, out):
+    other = 1 - core[0]
     out[...] = (keep[...] + received[other].astype(jnp.float32)).astype(out.dtype)
 
 
@@ -132,17 +132,20 @@
     share[...] = jnp.sum(both[:, n:].astype(jnp.float32), axis=0)
 
 
-def backward_kernel(meta, gathered, tiles, share, keep, send, block, acc):
+def backward_kernel(scalars, gathered, tiles, share, keep, send, block, acc, meta, sem):
+    copy = pltpu.make_async_copy(scalars, meta, sem)
+    copy.start()
     nrep, ncol, own_rows, feat = gathered.shape
     slots, tile = tiles.shape[0], tiles.shape[-1]
     pieces = tile // (own_rows * nrep)
-    me = meta[2 * slots + 1]
     for t in range(block.shape[0]):
         upstream = jnp.concatenate(
             [gathered[c, t * pieces + q] for q in range(pieces) for c in range(nrep)], axis=0
         )
         block[t] = upstream.T
     acc[...] = jnp.zeros_like(acc)
+    copy.wait()
+    me = meta[2 * slots + 1]
 
     def step(k):
         part = jnp.dot(block[meta[k]], tiles[k], preferred_element_type=jnp.float32)
@@ -155,21 +158,17 @@
     for t in range(acc.shape[0]):
         keep[t] = acc[t, me].T
         send[t * n : (t + 1) * n] = acc[t, 1 - me].T.astype(send.dtype)
-    half = own_rows // nrep
-    start = pl.multiple_of((1 - me) * half, half)
-    send[acc.shape[0] * n :] = share[pl.ds(start, half), :].astype(send.dtype)
-
-
-def merge_kernel(meta, keep, received, share, out):
-    me = meta[meta.shape[0] - 1]
+    send[acc.shape[0] * n :] = share[...].astype(send.dtype)
+
+
+def merge_kernel(core, keep, received, share, out):
+    other = 1 - core[0]
     nrow, n, _ = keep.shape
-    half = out.shape[1] - n
-    start = pl.multiple_of(me * half, half)
-    grad = share[pl.ds(start, half), :] + received[1 - me, nrow * n :].astype(jnp.float32)
+    grad = (share[...] + received[other, nrow * n :].astype(jnp.float32)).astype(out.dtype)
     for r in range(nrow):
-        part = received[1 - me, r * n : (r + 1) * n].astype(jnp.float32)
+        part = received[other, r * n : (r + 1) * n].astype(jnp.float32)
         out[r, :n] = (keep[r] + part).astype(out.dtype)
-        out[r, n:] = grad.astype(out.dtype)
+        out[r, n:] = grad
 
 
 def finish_kernel(parts, d_src, send):
@@ -181,15 +180,13 @@
 
 
 def weights_kernel(gathered, grad_self, grad_neigh):
-    nrep, ncol, share, feat = gathered.shape
-    per = feat // (share * nrep)
+    ncol, n, feat = gathered.shape
+    per = feat // n
     for j in range(ncol):
         lane, row = divmod(j, 2 * per)
         which, row = divmod(row, per)
         out = (grad_self, grad_neigh)[which]
-        for c in range(nrep):
-            start = (row * nrep + c) * share
-            out[start : start + share, lane * feat : (lane + 1) * feat] = gathered[c, j].astype(jnp.float32)
+        out[row * n : (row + 1) * n, lane * feat : (lane + 1) * feat] = gathered[j].astype(jnp.float32)
 
 
 def exchange(x, axis):
@@ -202,18 +199,11 @@
     f32, bf16 = jnp.float32, jnp.bfloat16
     nrow, ncol, nrep = lax.axis_size("row"), lax.axis_size("col"), lax.axis_size("rep")
     tiles = tile_vals.reshape(tile_vals.shape[3:])
-    meta = jnp.concatenate(
-        [
-            tile_rows.reshape(-1),
-            tile_cols.reshape(-1),
-            tile_count.reshape(-1),
-            lax.axis_index("rep").astype(jnp.int32).reshape(1),
-        ]
-    )
+    core = lax.axis_index("rep").astype(jnp.int32).reshape(1)
+    meta = jnp.concatenate([tile_rows.reshape(-1), tile_cols.reshape(-1), tile_count.reshape(-1), core])
     slots, tile = tiles.shape[:2]
     own_src, feat = x_src.shape[1:]
     own_rows = x_dst.shape[1]
-    half = own_rows // nrep
     hid = w_self.shape[1]
     row_tiles = own_rows * ncol * nrep // tile
     col_tiles = own_src * nrow * nrep // tile
@@ -226,9 +216,6 @@
         spread_kernel,
         shape((nrow, own_src, feat), bf16),
         (x_src,),
-        in_specs=[ANY],
-        out_specs=ANY,
-        scratch=(pltpu.SemaphoreType.DMA((nrow,)),),
     )
     source = exchange(source, "row")
     held = (tiles, degree, x_dst[0], cotangent[0], w_self, w_neigh)
@@ -245,10 +232,11 @@
         forward_kernel,
         (shape((ncol, own_rows, feat), f32), shape((ncol, own_rows, feat), bf16)),
         (meta, source, tiles),
-        in_specs=[SMEM, VMEM, VMEM],
         scratch=(
             pltpu.VMEM((own_src * nrow * nrep, feat), bf16),
             pltpu.VMEM((row_tiles, tile, feat), f32),
+            pltpu.SMEM(meta.shape, meta.dtype),
+            pltpu.SemaphoreType.DMA,
         ),
         cost=cost,
     )
@@ -256,7 +244,7 @@
     parts = call(
         add_kernel,
         shape((ncol, own_rows, feat), bf16),
-        (meta, keep, received),
+        (core, keep, received),
         in_specs=[SMEM, VMEM, VMEM],
     )
     parts = exchange(parts, "col")
@@ -277,28 +265,29 @@
     gathered = lax.all_gather(dagg, "rep", axis=0)
     keep, send = call(
         backward_kernel,
-        (shape((nrow, own_src, feat), f32), shape((nrow * own_src + half, feat), bf16)),
+        (shape((nrow, own_src, feat), f32), shape((nrow * own_src + own_rows, feat), bf16)),
         (meta, gathered, tiles, share),
-        in_specs=[SMEM] + [VMEM] * 3,
         scratch=(
             pltpu.VMEM((row_tiles, feat, tile), bf16),
             pltpu.VMEM((col_tiles, nrep, feat, tile // nrep), f32),
+            pltpu.SMEM(meta.shape, meta.dtype),
+            pltpu.SemaphoreType.DMA,
         ),
         cost=cost,
     )
     received = lax.all_gather(send, "rep", axis=0)
     merged = call(
         merge_kernel,
-        shape((nrow, own_src + half, feat), bf16),
-        (meta, keep, received, share),
+        shape((nrow, own_src + own_rows, feat), bf16),
+        (core, keep, received, share),
         in_specs=[SMEM] + [VMEM] * 3,
     )
     d_x_src, send = call(
         finish_kernel,
-        (shape((own_src, feat), bf16), shape((ncol, half, feat), bf16)),
+        (shape((own_src, feat), bf16), shape((ncol, own_rows, feat), bf16)),
         (exchange(merged, "row"),),
     )
-    shares = lax.all_gather(exchange(send, "col"), "rep", axis=0)
+    shares = exchange(send, "col")
     grad_self, grad_neigh = call(
         weights_kernel, (shape((feat, hid), f32), shape((feat, hid), f32)), (shares,)
     )

time: 124 us -> 120 us (0.968)
  blocking collectives: 93.8 us -> 91.1 us
    all_gather x1 -> x0, blocking collectives: 4.49 us -> none  [on_device(): shares = lax.all_gather(exchange(send, 'col'), 'rep', axis=0)]
where the time goes in v3:
time: 120 us; the launch traced here: 119 us
  blocking collectives  91.1 us (76%)
  starting transfers between devices  10.1 us (8%)
  Pallas kernels  6.98 us (6%)
  local copies, waits for them, and re-layouts  6.56 us (5%)
  waiting for transfers between devices  3.05 us (3%)
  between operations  1.36 us (1%)
    all_to_all x4, blocking collectives, exchange(): return lax.all_to_all(x, axis, split_axis=0, concat_axis=0, tiled=True)  76.9 us
    all_to_all x1, starting transfers between devices, exchange(): return lax.all_to_all(x, axis, split_axis=0, concat_axis=0, tiled=True)  10.1 us
    pallas_call x10, Pallas kernels, call(): pl.pallas_call(kernel, out_shape=out_shape, in_specs=in_specs or [VMEM] *...  6.98 us
    unnamed x18, local copies, waits for them, and re-layouts  6.56 us
    all_gather x1, blocking collectives, on_device(): gathered = lax.all_gather(dagg, 'rep', axis=0)  5.08 us
    all_gather x2, blocking collectives, on_device(): received = lax.all_gather(send, 'rep', axis=0)  5.06 us
    all_gather x1, blocking collectives, on_device(): source = lax.all_gather(source, 'rep', axis=0)  4.07 us
    all_to_all x1, waiting for transfers between devices, exchange(): return lax.all_to_all(x, axis, split_axis=0, concat_axis=0, tiled=True)  3.05 us
  transfers between devices with their start and end apart: 1, of which 1 were waited for; matrix products, arithmetic and copies ran while one was open for 0% of the time, Pallas kernels for 1%

profile of v3, /device:TPU:1, one launch (start us, length us, event | category | flops | bytes accessed | tf_op | source)
XLA Modules:
  0.0 119.2 jit_solution(18287763745125019504)
XLA Ops:
  0.6 0.0 copy-start.4
  0.6 0.7 copy-done.4
  1.4 0.0 copy-start.7
  1.4 0.0 copy-start.8
  1.4 0.7 shard_map.137
  2.1 10.1 %all-to-all-start = ((bf16[8,128,128]{2,1,0:T(8,128)(2,1)}), bf16[8,128,128]{2,1,0:T(8,128)(2,1)}, u32[]{:S(2)}, u32[]{:S(2)}) async-start(bf16[8,128,128]{2,1,0:T(8,128)(2,1)} %shard_map.137), calls=%async_computation | async-start | bytes 524288 | tf_op jit(solution)/shard_map/all_to_all | solution.py:193
  12.9 0.0 copy-start
  12.9 1.9 %copy-done = bf16[1,1,1,24,256,256]{5,4,3,2,1,0:T(8,128)(2,1)S(1)} copy-done((bf16[1,1,1,24,256,256]{5,4,3,2,1,0:T(8,128)(2,1)S(1)}, bf16[1,1,1,24,256,256]{5,4,3,2,1,0:T(8,128)(2,1)}, u32[]{:S(2)}) %copy-start) | copy-done | bytes 3145752
  14.8 0.0 copy-start.1
  14.8 0.9 copy-done.1
  15.7 0.0 copy-start.2
  15.7 0.9 copy-done.2
  16.6 0.0 copy-start.3
  16.6 0.8 copy-done.3
  17.4 0.0 copy-start.5
  17.4 0.7 copy-done.5
  18.1 0.0 copy-start.6
  18.1 0.7 copy-done.6
  18.7 0.7 shard_map.138
  19.4 0.0 copy-done.7
  19.4 0.0 copy-done.8
  19.4 0.1 pad_add_fusion.scalars
  19.5 3.1 %all-to-all-done = bf16[8,128,128]{2,1,0:T(8,128)(2,1)} async-done(((bf16[8,128,128]{2,1,0:T(8,128)(2,1)}), bf16[8,128,128]{2,1,0:T(8,128)(2,1)}, u32[]{:S(2)}, u32[]{:S(2)}) %all-to-all-start) | async-done | bytes 262176 | tf_op jit(solution)/shard_map/all_to_all | solution.py:193
  22.5 4.1 %all-gather = bf16[16,128,128]{2,1,0:T(8,128)(2,1)S(1)} all-gather(bf16[8,128,128]{2,1,0:T(8,128)(2,1)} %all-to-all-done), channel_id=2, replica_groups=mesh['row'=8,'col'=32,'rep'=2] {'rep'}, dimensions={0}, use_global_device_ids=true | all-gather | bytes 786432 | tf_op jit(solution)/shard_map/all_gather | solution.py:230
  26.6 1.3 %shard_map.139 = (f32[32,32,128]{2,1,0:T(8,128)S(1)}, bf16[32,32,128]{2,1,0:T(8,128)(2,1)S(1)}) custom-call(s32[50]{0:T(128)S(1)} %pad_add_fusion.scalars, bf16[2,8,128,128]{3,2,1,0:T(8,128)(2,1)S(1)} %bitcast.19, bf16[24,256,256]{2,1,0:T(8,128)(2,1)S(1)} %get-tuple-element.24.tiles), custom_call_target="tpu_custom_call" | custom-call | flops 402653184 | bytes 3145728 | tf_op jit(solution)/shard_map/pallas_call | solution.py:17
  27.9 2.5 %all-gather.1 = bf16[64,32,128]{2,1,0:T(8,128)(2,1)S(1)} all-gather(bf16[32,32,128]{2,1,0:T(8,128)(2,1)S(1)} %get-tuple-element.26), channel_id=3, replica_groups=mesh['row'=8,'col'=32,'rep'=2] {'rep'}, dimensions={0}, use_global_device_ids=true | all-gather | bytes 786432 | tf_op jit(solution)/shard_map/all_gather | solution.py:243
  30.5 0.1 shard_map.140
  30.5 25.0 %all_to_all.25.parts = bf16[32,32,128]{2,1,0:T(8,128)(2,1)S(1)} all-to-all(bf16[32,32,128]{2,1,0:T(8,128)(2,1)S(1)} %shard_map.140), channel_id=1, replica_groups=mesh['row'=8,'col'=32,'rep'=2] {'col'}, dimensions={0} | all-to-all | bytes 524288 | tf_op jit(solution)/shard_map/all_to_all | solution.py:193
  55.6 1.1 shard_map.141
  56.6 19.5 %all_to_all.26.both = bf16[32,64,128]{2,1,0:T(8,128)(2,1)S(1)} all-to-all(bf16[32,64,128]{2,1,0:T(8,128)(2,1)S(1)} %get-tuple-element.33), channel_id=1, replica_groups=mesh['row'=8,'col'=32,'rep'=2] {'col'}, dimensions={0} | all-to-all | bytes 1048576 | tf_op jit(solution)/shard_map/all_to_all | solution.py:193
  76.2 0.1 shard_map.142
  76.2 5.1 %all-gather.2 = bf16[64,32,128]{2,1,0:T(8,128)(2,1)S(1)} all-gather(bf16[32,32,128]{2,1,0:T(8,128)(2,1)S(1)} %get-tuple-element.34), channel_id=4, replica_groups=mesh['row'=8,'col'=32,'rep'=2] {'rep'}, dimensions={0}, use_global_device_ids=true | all-gather | bytes 786432 | tf_op jit(solution)/shard_map/all_gather | solution.py:265
  81.3 1.5 %shard_map.143 = (f32[8,128,128]{2,1,0:T(8,128)S(1)}, bf16[1056,128]{1,0:T(8,128)(2,1)S(1)}) custom-call(s32[50]{0:T(128)S(1)} %pad_add_fusion.scalars, bf16[2,32,32,128]{3,2,1,0:T(8,128)(2,1)S(1)} %bitcast.18, bf16[24,256,256]{2,1,0:T(8,128)(2,1)S(1)} %get-tuple-element.24.tiles, f32[32,128]{1,0:T(8,128)S(1)} %get-tuple-element.35.share), custom_call_target="tpu_custom_call" | custom-call | flops 402653184 | bytes 3145728 | tf_op jit(solution)/shard_map/pallas_call | solution.py:17
  82.8 2.5 %all-gather.3 = bf16[2112,128]{1,0:T(8,128)(2,1)S(1)} all-gather(bf16[1056,128]{1,0:T(8,128)(2,1)S(1)} %get-tuple-element.37), channel_id=5, replica_groups=mesh['row'=8,'col'=32,'rep'=2] {'rep'}, dimensions={0}, use_global_device_ids=true | all-gather | bytes 811008 | tf_op jit(solution)/shard_map/all_gather | solution.py:278
  85.4 13.9 %all_to_all.27.parts = bf16[8,160,128]{2,1,0:T(8,128)(2,1)S(1)} all-to-all(bf16[8,160,128]{2,1,0:T(8,128)(2,1)S(1)} %shard_map.144), channel_id=1, replica_groups=mesh['row'=8,'col'=32,'rep'=2] {'row'}, dimensions={0} | all-to-all | bytes 655360 | tf_op jit(solution)/shard_map/all_to_all | solution.py:193
  99.3 0.7 shard_map.145
  100.0 18.4 %all_to_all.28.gathered = bf16[32,32,128]{2,1,0:T(8,128)(2,1)S(1)} all-to-all(bf16[32,32,128]{2,1,0:T(8,128)(2,1)S(1)} %get-tuple-element.40), channel_id=1, replica_groups=mesh['row'=8,'col'=32,'rep'=2] {'col'}, dimensions={0} | all-to-all | bytes 524288 | tf_op jit(solution)/shard_map/all_to_all | solution.py:193
  118.3 0.8 shard_map.146
  (1 shorter events, 0.0 us)
Async XLA Ops:
  0.6 0.8 copy-start.4
  1.4 18.0 %copy-start.7 = (s32[1,1,1,24]{3,2,1,0:T(1,128)S(1)}, s32[1,1,1,24]{3,2,1,0:T(1,128)}, u32[]{:S(2)}) copy-start(s32[1,1,1,24]{3,2,1,0:T(1,128)} %param.15) | copy-start | bytes 292
  1.4 18.0 %copy-start.8 = (s32[1,1,1,24]{3,2,1,0:T(1,128)S(1)}, s32[1,1,1,24]{3,2,1,0:T(1,128)}, u32[]{:S(2)}) copy-start(s32[1,1,1,24]{3,2,1,0:T(1,128)} %param.14) | copy-start | bytes 292
  2.1 20.4 %all-to-all-start = ((bf16[8,128,128]{2,1,0:T(8,128)(2,1)}), bf16[8,128,128]{2,1,0:T(8,128)(2,1)}, u32[]{:S(2)}, u32[]{:S(2)}) async-start(bf16[8,128,128]{2,1,0:T(8,128)(2,1)} %shard_map.137), calls=%async_computation | async-start | bytes 524288 | tf_op jit(solution)/shard_map/all_to_all | solution.py:193
  12.9 1.9 %copy-start = (bf16[1,1,1,24,256,256]{5,4,3,2,1,0:T(8,128)(2,1)S(1)}, bf16[1,1,1,24,256,256]{5,4,3,2,1,0:T(8,128)(2,1)}, u32[]{:S(2)}) copy-start(bf16[1,1,1,24,256,256]{5,4,3,2,1,0:T(8,128)(2,1)} %param.13) | copy-start | bytes 9437188
  14.8 0.9 copy-start.1
  15.7 0.9 copy-start.2
  16.6 0.8 copy-start.3
  17.4 0.7 copy-start.5
  18.1 0.7 copy-start.6

commit v4 on v3

v4 whole, which is shorter than its diff:
```python
import jax
import jax.numpy as jnp
from jax import lax
from jax.experimental import pallas as pl
from jax.experimental.pallas import tpu as pltpu
from jax.sharding import PartitionSpec as P

GELU_SCALE = 0.7978845608
GELU_CUBE = 0.044715
MIB = 1 << 20
VMEM = pl.BlockSpec(memory_space=pltpu.VMEM)
HBM = pl.BlockSpec(memory_space=pltpu.HBM)


def in_hbm(x):
    return pltpu.with_memory_space_constraint(x, pltpu.HBM)


def call(kernel, out_shape, operands, in_specs=None, out_specs=None, scratch=(), limit=16, cost=None):
    return pl.pallas_call(
        kernel,
        out_shape=out_shape,
        in_specs=in_specs or [VMEM] * len(operands),
        out_specs=out_specs or jax.tree.map(lambda _: VMEM, out_shape),
        scratch_shapes=list(scratch),
        compiler_params=pltpu.CompilerParams(vmem_limit_bytes=limit * MIB),
        cost_estimate=cost,
    )(*operands)


def each_live(count, step, group=8):
    def many(g, carry):
        for u in range(group):
            step(g * group + u)
        return carry

    def one(k, carry):
        step(k)
        return carry

    groups = count // group
    lax.fori_loop(0, groups, many, 0)
    lax.fori_loop(groups * group, count, one, 0)


def spread_kernel(x, out, held, sem):
    copy = pltpu.make_async_copy(x, held, sem)
    copy.start()
    copy.wait()
    for r in range(out.shape[0]):
        out[r] = held[0]


def fetch_kernel(
    rows_in, cols_in, count_in, tiles_in, deg_in, own_in, cot_in, w_self_in, w_neigh_in,
    rows, cols, count, tiles, degree, own, pre, cot, w_neigh, down_self, down_neigh,
    deg, feats, w_self, sems,
):
    pairs = (
        (own_in, feats), (w_self_in, w_self), (w_neigh_in, w_neigh), (deg_in, deg),
        (rows_in, rows), (cols_in, cols), (cot_in, cot), (tiles_in, tiles),
    )
    copies = [pltpu.make_async_copy(x, y, sems.at[i]) for i, (x, y) in enumerate(pairs)]
    for copy in copies:
        copy.start()
    count[...] = jnp.broadcast_to(count_in[0], count.shape)
    for copy in copies[:4]:
        copy.wait()
    n = own.shape[1]
    along = jnp.broadcast_to(deg[...].astype(jnp.float32), (n, n))
    diagonal = lax.broadcasted_iota(jnp.int32, (n, n), 0) == lax.broadcasted_iota(jnp.int32, (n, n), 1)
    degree[...] = jnp.sum(jnp.where(diagonal, along, 0.0), axis=1, keepdims=True)
    own[...] = feats[0].T
    pre[...] = jnp.dot(feats[0], w_self[...], preferred_element_type=jnp.float32)
    down_self[...] = w_self[...].T
    down_neigh[...] = w_neigh[...].T
    for copy in copies[4:]:
        copy.wait()


def load_scalars(sources, targets, sems):
    copies = [pltpu.make_async_copy(x, y, sems.at[i]) for i, (x, y) in enumerate(zip(sources, targets))]
    for copy in copies:
        copy.start()

    def wait():
        for copy in copies:
            copy.wait()

    return wait


def forward_kernel(
    rows_in, cols_in, count_in, source, tiles, keep, send, block, acc, rows, cols, count, sems
):
    wait = load_scalars((rows_in, cols_in, count_in), (rows, cols, count), sems)
    nrep, nrow, part, _ = source.shape
    tile = tiles.shape[-1]
    own_rows = keep.shape[1]
    for r in range(nrow):
        for c in range(nrep):
            block[pl.ds((r * nrep + c) * part, part), :] = source[c, r]
    acc[...] = jnp.zeros_like(acc)
    wait()

    def step(k):
        start = pl.multiple_of(cols[k] * tile, tile)
        acc[rows[k]] += jnp.dot(
            tiles[k], block[pl.ds(start, tile), :], preferred_element_type=jnp.float32
        )

    each_live(count[0, 0], step)
    me = lax.axis_index("rep")
    pieces = tile // (own_rows * nrep)
    for t in range(acc.shape[0]):
        for q in range(pieces):
            base = q * nrep * own_rows
            mine = pl.multiple_of(base + me * own_rows, own_rows)
            other = pl.multiple_of(base + (1 - me) * own_rows, own_rows)
            keep[t * pieces + q] = acc[t, pl.ds(mine, own_rows), :]
            send[t * pieces + q] = acc[t, pl.ds(other, own_rows), :].astype(send.dtype)


def add_kernel(keep, received, out):
    other = 1 - lax.axis_index("rep")
    out[...] = (keep[...] + received[other].astype(jnp.float32)).astype(out.dtype)


def dense_kernel(parts, deg, own, pre_self, cotangent, w_neigh, down_self, down_neigh, hidden, d_own, send):
    agg = jnp.sum(parts[...].astype(jnp.float32), axis=0)
    degree = deg[...]
    neigh = (agg / degree).astype(jnp.bfloat16)
    pre = pre_self[...] + jnp.dot(neigh, w_neigh[...], preferred_element_type=jnp.float32)
    square = pre * pre
    t = jnp.tanh(GELU_SCALE * (pre + GELU_CUBE * (pre * square)))
    half = 0.5 * (1.0 + t)
    hidden[...] = (pre * half).astype(hidden.dtype)
    slope = half + 0.5 * pre * (1.0 - t * t) * (GELU_SCALE * (1.0 + 3.0 * GELU_CUBE * square))
    dpre = (cotangent[0].astype(jnp.float32) * slope).astype(jnp.bfloat16)
    d_own[...] = jnp.dot(dpre, down_self[...], preferred_element_type=jnp.float32).astype(d_own.dtype)
    dagg = jnp.dot(dpre, down_neigh[...], preferred_element_type=jnp.float32) / degree
    dagg = dagg.astype(send.dtype)
    grads = [
        jnp.dot(lhs, dpre, preferred_element_type=jnp.float32).astype(send.dtype) for lhs in (own[...], neigh.T)
    ]
    feat, n = own.shape
    per = feat // n
    for j in range(send.shape[0]):
        lane, row = divmod(j, 2 * per)
        which, row = divmod(row, per)
        send[j, :n] = dagg
        send[j, n:] = grads[which][row * n : (row + 1) * n, lane * feat : (lane + 1) * feat]


def split_kernel(both, dagg, share):
    n = dagg.shape[1]
    dagg[...] = both[:, :n]
    share[...] = jnp.sum(both[:, n:].astype(jnp.float32), axis=0)


def backward_kernel(
    rows_in, cols_in, count_in, gathered, tiles, share, keep, send, block, acc, rows, cols, count, sems
):
    wait = load_scalars((rows_in, cols_in, count_in), (rows, cols, count), sems)
    nrep, ncol, own_rows, feat = gathered.shape
    tile = tiles.shape[-1]
    pieces = tile // (own_rows * nrep)
    for t in range(block.shape[0]):
        upstream = jnp.concatenate(
            [gathered[c, t * pieces + q] for q in range(pieces) for c in range(nrep)], axis=0
        )
        block[t] = upstream.T
    acc[...] = jnp.zeros_like(acc)
    wait()
    me = lax.axis_index("rep")

    def step(k):
        part = jnp.dot(block[rows[k]], tiles[k], preferred_element_type=jnp.float32)
        where = cols[k]
        for c in range(nrep):
            acc[where, c] += part[:, c * feat : (c + 1) * feat]

    each_live(count[0, 0], step)
    n = keep.shape[1]
    for t in range(acc.shape[0]):
        keep[t] = acc[t, me].T
        send[t * n : (t + 1) * n] = acc[t, 1 - me].T.astype(send.dtype)
    send[acc.shape[0] * n :] = share[...].astype(send.dtype)


def merge_kernel(keep, received, share, out):
    other = 1 - lax.axis_index("rep")
    nrow, n, _ = keep.shape
    grad = (share[...] + received[other, nrow * n :].astype(jnp.float32)).astype(out.dtype)
    for r in range(nrow):
        part = received[other, r * n : (r + 1) * n].astype(jnp.float32)
        out[r, :n] = (keep[r] + part).astype(out.dtype)
        out[r, n:] = grad


def total_kernel(parts, send):
    n = parts.shape[1] - send.shape[1]
    share = jnp.sum(parts[:, n:].astype(jnp.float32), axis=0).astype(send.dtype)
    for j in range(send.shape[0]):
        send[j] = share


def finish_kernel(gathered, parts, hidden_in, d_own_in, hidden, d_src, d_own, grad_self, grad_neigh):
    ncol, n, feat = gathered.shape
    per = feat // n
    for j in range(ncol):
        lane, row = divmod(j, 2 * per)
        which, row = divmod(row, per)
        out = (grad_self, grad_neigh)[which]
        out[row * n : (row + 1) * n, lane * feat : (lane + 1) * feat] = gathered[j].astype(jnp.float32)
    d_src[0] = jnp.sum(parts[:, : d_src.shape[1]].astype(jnp.float32), axis=0).astype(d_src.dtype)
    hidden[0] = hidden_in[...]
    d_own[0] = d_own_in[...]


def exchange(x, axis):
    return lax.all_to_all(x, axis, split_axis=0, concat_axis=0, tiled=True)


def on_device(
    x_src, x_dst, degree, tile_vals, tile_rows, tile_cols, tile_count, w_self, w_neigh, cotangent
):
    f32, bf16 = jnp.float32, jnp.bfloat16
    nrow, ncol, nrep = lax.axis_size("row"), lax.axis_size("col"), lax.axis_size("rep")
    tiles = tile_vals.reshape(tile_vals.shape[3:])
    slots, tile = tiles.shape[:2]
    own_src, feat = x_src.shape[1:]
    own_rows = x_dst.shape[1]
    hid = w_self.shape[1]
    row_tiles = own_rows * ncol * nrep // tile
    col_tiles = own_src * nrow * nrep // tile
    shape = jax.ShapeDtypeStruct
    cost = pl.CostEstimate(
        flops=2 * slots * tile * tile * feat, bytes_accessed=tiles.size * 2, transcendentals=0
    )

    source = call(
        spread_kernel,
        shape((nrow, own_src, feat), bf16),
        (in_hbm(x_src),),
        in_specs=[HBM],
        scratch=(pltpu.VMEM(x_src.shape, bf16), pltpu.SemaphoreType.DMA),
    )
    source = exchange(source, "row")
    places = (tile_rows.reshape(-1), tile_cols.reshape(-1))
    inputs = (tiles, degree, x_dst, cotangent, w_self, w_neigh)
    rows, cols, count, tiles, *held = call(
        fetch_kernel,
        (
            *(shape(x.shape, x.dtype) for x in places),
            shape((8, 128), jnp.int32),
            shape(tiles.shape, bf16),
            shape((own_rows, 1), f32),
            shape((feat, own_rows), bf16),
            shape((own_rows, hid), f32),
            shape(cotangent.shape, bf16),
            shape((feat, hid), bf16),
            shape((hid, feat), bf16),
            shape((hid, feat), bf16),
        ),
        (*map(in_hbm, places), tile_count, *map(in_hbm, inputs)),
        in_specs=[HBM, HBM, VMEM] + [HBM] * len(inputs),
        scratch=(
            pltpu.VMEM(degree.shape, degree.dtype),
            pltpu.VMEM(x_dst.shape, bf16),
            pltpu.VMEM(w_self.shape, bf16),
            pltpu.SemaphoreType.DMA((8,)),
        ),
        cost=pl.CostEstimate(flops=0, bytes_accessed=tiles.size * 4, transcendentals=0),
    )
    scalars = (rows, cols, count)
    source = lax.all_gather(source, "rep", axis=0)
    keep, send = call(
        forward_kernel,
        (shape((ncol, own_rows, feat), f32), shape((ncol, own_rows, feat), bf16)),
        (*scalars, source, tiles),
        scratch=(
            pltpu.VMEM((own_src * nrow * nrep, feat), bf16),
            pltpu.VMEM((row_tiles, tile, feat), f32),
            *(pltpu.SMEM(x.shape, x.dtype) for x in scalars),
            pltpu.SemaphoreType.DMA((len(scalars),)),
        ),
        cost=cost,
    )
    received = lax.all_gather(send, "rep", axis=0)
    parts = call(
        add_kernel,
        shape((ncol, own_rows, feat), bf16),
        (keep, received),
    )
    parts = exchange(parts, "col")
    hidden, d_x_dst, send = call(
        dense_kernel,
        (
            shape((own_rows, hid), bf16),
            shape((own_rows, feat), bf16),
            shape((ncol, 2 * own_rows, feat), bf16),
        ),
        (parts, *held),
    )
    dagg, share = call(
        split_kernel,
        (shape((ncol, own_rows, feat), bf16), shape((own_rows, feat), f32)),
        (exchange(send, "col"),),
    )
    gathered = lax.all_gather(dagg, "rep", axis=0)
    keep, send = call(
        backward_kernel,
        (shape((nrow, own_src, feat), f32), shape((nrow * own_src + own_rows, feat), bf16)),
        (*scalars, gathered, tiles, share),
        scratch=(
            pltpu.VMEM((row_tiles, feat, tile), bf16),
            pltpu.VMEM((col_tiles, nrep, feat, tile // nrep), f32),
            *(pltpu.SMEM(x.shape, x.dtype) for x in scalars),
            pltpu.SemaphoreType.DMA((len(scalars),)),
        ),
        cost=cost,
    )
    received = lax.all_gather(send, "rep", axis=0)
    merged = call(
        merge_kernel,
        shape((nrow, own_src + own_rows, feat), bf16),
        (keep, received, share),
    )
    parts = exchange(merged, "row")
    send = call(total_kernel, shape((ncol, own_rows, feat), bf16), (parts,))
    return call(
        finish_kernel,
        (
            shape((1, own_rows, hid), bf16),
            shape((1, own_src, feat), bf16),
            shape((1, own_rows, feat), bf16),
            shape((feat, hid), f32),
            shape((feat, hid), f32),
        ),
        (exchange(send, "col"), parts, hidden, d_x_dst),
    )


def solution(mesh):
    return jax.shard_map(
        on_device,
        mesh=mesh,
        in_specs=(
            P("col", ("row", "rep"), None),
            P("row", ("col", "rep"), None),
            P("row", ("col", "rep")),
            P("row", "col", "rep", None, None, None),
            P("row", "col", "rep", None),
            P("row", "col", "rep", None),
            P("row", "col", "rep"),
            P(),
            P(),
            P("row", ("col", "rep"), None),
        ),
        out_specs=(
            P("row", ("col", "rep"), None),
            P("col", ("row", "rep"), None),
            P("row", ("col", "rep"), None),
            P(),
            P(),
        ),
        check_vma=False,
    )
```

time: 120 us -> 119 us (level)
  local copies, waits for them, and re-layouts: 6.56 us -> 2.46 us
  Pallas kernels: 6.98 us -> 9.13 us
  waiting for transfers between devices: 3.05 us -> 4.96 us
    unnamed x18 -> x16, local copies, waits for them, and re-layouts: 6.56 us -> 2.46 us
    pallas_call x10, Pallas kernels: 6.98 us -> 9.13 us  [call(): pl.pallas_call(kernel, out_shape=out_shape, in_specs=in_specs or [VMEM] *...]
    all_to_all x1, waiting for transfers between devices: 3.05 us -> 4.96 us  [exchange(): return lax.all_to_all(x, axis, split_axis=0, concat_axis=0, tiled=True)]
  transfers between devices with their start and end apart: 1 -> 1, of which waited for: 1 -> 1; matrix products, arithmetic and copies ran while one was open for 0% -> 0% of each run, Pallas kernels for 1% -> 2%
where the time goes in v4:
time: 119 us; the launch traced here: 118 us
  blocking collectives  90.4 us (76%)
  starting transfers between devices  10.1 us (8%)
  Pallas kernels  9.13 us (8%)
  waiting for transfers between devices  4.96 us (4%)
  local copies, waits for them, and re-layouts  2.46 us (2%)
  between operations  1.37 us (1%)
    all_to_all x4, blocking collectives, exchange(): return lax.all_to_all(x, axis, split_axis=0, concat_axis=0, tiled=True)  76.8 us
    all_to_all x1, starting transfers between devices, exchange(): return lax.all_to_all(x, axis, split_axis=0, concat_axis=0, tiled=True)  10.1 us
    pallas_call x10, Pallas kernels, call(): pl.pallas_call(kernel, out_shape=out_shape, in_specs=in_specs or [VMEM] *...  9.13 us
    all_gather x1, blocking collectives, on_device(): gathered = lax.all_gather(dagg, 'rep', axis=0)  5.09 us
    all_to_all x1, waiting for transfers between devices, exchange(): return lax.all_to_all(x, axis, split_axis=0, concat_axis=0, tiled=True)  4.96 us
    all_gather x2, blocking collectives, on_device(): received = lax.all_gather(send, 'rep', axis=0)  4.38 us
    all_gather x1, blocking collectives, on_device(): source = lax.all_gather(source, 'rep', axis=0)  4.07 us
    unnamed x16, local copies, waits for them, and re-layouts  2.46 us
  transfers between devices with their start and end apart: 1, of which 1 were waited for; matrix products, arithmetic and copies ran while one was open for 0% of the time, Pallas kernels for 2%

profile of v4, /device:TPU:1, one launch (start us, length us, event | category | flops | bytes accessed | tf_op | source)
XLA Modules:
  0.0 118.4 jit_solution(7548048084754965831)
XLA Ops:
  0.6 1.5 %shard_map.138 = bf16[8,128,128]{2,1,0:T(8,128)(2,1)} custom-call(bf16[1,128,128]{2,1,0:T(8,128)(2,1)} %x.1), custom_call_target="tpu_custom_call" | custom-call | tf_op jit(solution)/shard_map/pallas_call | solution.py:20
  2.1 10.1 %all-to-all-start = ((bf16[8,128,128]{2,1,0:T(8,128)(2,1)}), bf16[8,128,128]{2,1,0:T(8,128)(2,1)}, u32[]{:S(2)}, u32[]{:S(2)}) async-start(bf16[8,128,128]{2,1,0:T(8,128)(2,1)} %shard_map.138), calls=%async_computation | async-start | bytes 524288 | tf_op jit(solution)/shard_map/all_to_all | solution.py:222
  12.9 2.2 %shard_map.137 = (s32[24]{0:T(128)S(1)}, s32[24]{0:T(128)S(1)}, s32[8,128]{1,0:T(8,128)S(1)}, bf16[24,256,256]{2,1,0:T(8,128)(2,1)S(1)}, f32[32,1]{1,0:T(8,128)S...) custom-call(s32[24]{0:T(128)} %bitcast.12, ...), custom_call_target="tpu_custom_call" | custom-call | bytes 6291456 | tf_op jit(solution)/shard_map/pallas_call | solution.py:20
  15.1 0.0 copy-start
  15.1 0.6 copy-done
  15.8 0.0 copy-start.2
  15.8 0.6 copy-done.2
  16.4 0.0 copy-start.4
  16.4 0.6 copy-done.4
  17.0 0.0 copy-start.6
  17.0 0.6 copy-done.6
  17.6 5.0 %all-to-all-done = bf16[8,128,128]{2,1,0:T(8,128)(2,1)} async-done(((bf16[8,128,128]{2,1,0:T(8,128)(2,1)}), bf16[8,128,128]{2,1,0:T(8,128)(2,1)}, u32[]{:S(2)}, u32[]{:S(2)}) %all-to-all-start) | async-done | bytes 262176 | tf_op jit(solution)/shard_map/all_to_all | solution.py:222
  22.5 4.1 %all-gather = bf16[16,128,128]{2,1,0:T(8,128)(2,1)S(1)} all-gather(bf16[8,128,128]{2,1,0:T(8,128)(2,1)} %all-to-all-done), channel_id=2, replica_groups=mesh['row'=8,'col'=32,'rep'=2] {'rep'}, dimensions={0}, use_global_device_ids=true | all-gather | bytes 786432 | tf_op jit(solution)/shard_map/all_gather | solution.py:277
  26.6 0.0 copy-start.1
  26.6 0.0 copy-start.3
  26.6 0.0 copy-start.5
  26.6 0.0 copy-start.7
  26.6 2.0 %shard_map.139 = (f32[32,32,128]{2,1,0:T(8,128)S(1)}, bf16[32,32,128]{2,1,0:T(8,128)(2,1)S(1)}) custom-call(s32[24]{0:T(128)S(1)} %get-tuple-element.25.rows_in, s32[24]{0:T(128)S(1)} %get-tuple-element.26.cols_in, s32[8,128]{1,0:T(8,128)S(1)} %get-tuple-element.27.count_in, bf16[2,8,128,128]{3,2,1,0:T(8,128)(2,1)S(1)} %bitcast.9, ...), custom_call_target="tpu_custom_call" | custom-call | flops 402653184 | bytes 3145728 | tf_op jit(solution)/shard_map/pallas_call | solution.py:20
  28.7 2.2 %all-gather.1 = bf16[64,32,128]{2,1,0:T(8,128)(2,1)S(1)} all-gather(bf16[32,32,128]{2,1,0:T(8,128)(2,1)S(1)} %get-tuple-element.30), channel_id=3, replica_groups=mesh['row'=8,'col'=32,'rep'=2] {'rep'}, dimensions={0}, use_global_device_ids=true | all-gather | bytes 786432 | tf_op jit(solution)/shard_map/all_gather | solution.py:290
  30.9 24.8 %all_to_all.25.parts = bf16[32,32,128]{2,1,0:T(8,128)(2,1)S(1)} all-to-all(bf16[32,32,128]{2,1,0:T(8,128)(2,1)S(1)} %shard_map.140), channel_id=1, replica_groups=mesh['row'=8,'col'=32,'rep'=2] {'col'}, dimensions={0} | all-to-all | bytes 524288 | tf_op jit(solution)/shard_map/all_to_all | solution.py:222
  55.7 0.0 copy-done.1
  55.7 0.0 copy-done.3
  55.7 0.0 copy-done.5
  55.7 0.0 copy-done.7
  55.7 0.5 shard_map.141
  56.2 19.5 %all_to_all.26.both = bf16[32,64,128]{2,1,0:T(8,128)(2,1)S(1)} all-to-all(bf16[32,64,128]{2,1,0:T(8,128)(2,1)S(1)} %get-tuple-element.38), channel_id=1, replica_groups=mesh['row'=8,'col'=32,'rep'=2] {'col'}, dimensions={0} | all-to-all | bytes 1048576 | tf_op jit(solution)/shard_map/all_to_all | solution.py:222
  75.7 0.1 shard_map.142
  75.8 5.1 %all-gather.2 = bf16[64,32,128]{2,1,0:T(8,128)(2,1)S(1)} all-gather(bf16[32,32,128]{2,1,0:T(8,128)(2,1)S(1)} %get-tuple-element.39), channel_id=4, replica_groups=mesh['row'=8,'col'=32,'rep'=2] {'rep'}, dimensions={0}, use_global_device_ids=true | all-gather | bytes 786432 | tf_op jit(solution)/shard_map/all_gather | solution.py:311
  80.9 1.9 %shard_map.143 = (f32[8,128,128]{2,1,0:T(8,128)S(1)}, bf16[1056,128]{1,0:T(8,128)(2,1)S(1)}) custom-call(s32[24]{0:T(128)S(1)} %get-tuple-element.25.rows_in, s32[24]{0:T(128)S(1)} %get-tuple-element.26.cols_in, s32[8,128]{1,0:T(8,128)S(1)} %get-tuple-element.27.count_in, bf16[2,32,32,128]{3,2,1,0:T(8,128)(2,1)S(1)} %bitcast.8, ...), custom_call_target="tpu_custom_call" | custom-call | flops 402653184 | bytes 3145728 | tf_op jit(solution)/shard_map/pallas_call | solution.py:20
  82.7 2.2 %all-gather.3 = bf16[2112,128]{1,0:T(8,128)(2,1)S(1)} all-gather(bf16[1056,128]{1,0:T(8,128)(2,1)S(1)} %get-tuple-element.42), channel_id=5, replica_groups=mesh['row'=8,'col'=32,'rep'=2] {'rep'}, dimensions={0}, use_global_device_ids=true | all-gather | bytes 811008 | tf_op jit(solution)/shard_map/all_gather | solution.py:324
  85.0 0.1 shard_map.144
  85.0 13.9 %all_to_all.27.parts = bf16[8,160,128]{2,1,0:T(8,128)(2,1)S(1)} all-to-all(bf16[8,160,128]{2,1,0:T(8,128)(2,1)S(1)} %shard_map.144), channel_id=1, replica_groups=mesh['row'=8,'col'=32,'rep'=2] {'row'}, dimensions={0} | all-to-all | bytes 655360 | tf_op jit(solution)/shard_map/all_to_all | solution.py:222
  98.9 18.6 %all_to_all.28.gathered = bf16[32,32,128]{2,1,0:T(8,128)(2,1)S(1)} all-to-all(bf16[32,32,128]{2,1,0:T(8,128)(2,1)S(1)} %shard_map.145), channel_id=1, replica_groups=mesh['row'=8,'col'=32,'rep'=2] {'col'}, dimensions={0} | all-to-all | bytes 524288 | tf_op jit(solution)/shard_map/all_to_all | solution.py:222
  117.6 0.9 shard_map.146
  (2 shorter events, 0.1 us)
Async XLA Ops:
  2.1 20.4 %all-to-all-start = ((bf16[8,128,128]{2,1,0:T(8,128)(2,1)}), bf16[8,128,128]{2,1,0:T(8,128)(2,1)}, u32[]{:S(2)}, u32[]{:S(2)}) async-start(bf16[8,128,128]{2,1,0:T(8,128)(2,1)} %shard_map.138), calls=%async_computation | async-start | bytes 524288 | tf_op jit(solution)/shard_map/all_to_all | solution.py:222
  15.1 0.6 copy-start
  15.8 0.6 copy-start.2
  16.4 0.6 copy-start.4
  17.0 0.6 copy-start.6
  26.6 29.1 %copy-start.1 = (f32[32,512]{1,0:T(8,128)S(1)}, f32[32,512]{1,0:T(8,128)}, u32[]{:S(2)}) copy-start(f32[32,512]{1,0:T(8,128)} %copy-done) | copy-start | bytes 196612
  26.6 29.1 %copy-start.3 = (bf16[128,32]{1,0:T(8,128)(2,1)S(1)}, bf16[128,32]{1,0:T(8,128)(2,1)}, u32[]{:S(2)}) copy-start(bf16[128,32]{1,0:T(8,128)(2,1)} %copy-done.2) | copy-start | bytes 24580
  26.6 29.1 %copy-start.5 = (bf16[1,32,512]{2,1,0:T(8,128)(2,1)S(1)}, bf16[1,32,512]{2,1,0:T(8,128)(2,1)}, u32[]{:S(2)}) copy-start(bf16[1,32,512]{2,1,0:T(8,128)(2,1)} %copy-done.4) | copy-start | bytes 98308
  26.6 29.1 %copy-start.7 = (f32[32,1]{1,0:T(8,128)S(1)}, f32[32,1]{1,0:T(8,128)}, u32[]{:S(2)}) copy-start(f32[32,1]{1,0:T(8,128)} %copy-done.6) | copy-start | bytes 388

commit v5 on v4

--- a/solution.py
+++ b/solution.py
@@ -8,6 +8,8 @@
 GELU_SCALE = 0.7978845608
 GELU_CUBE = 0.044715
 MIB = 1 << 20
+CODE_SCALE = 2.0**12
+CODE_FLOOR = 2.0**-120
 VMEM = pl.BlockSpec(memory_space=pltpu.VMEM)
 HBM = pl.BlockSpec(memory_space=pltpu.HBM)
 
@@ -90,6 +92,19 @@
     return wait
 
 
+def to_code(x):
+    y = x * CODE_SCALE
+    return (y * jnp.abs(y) * (y * y)).astype(jnp.bfloat16)
+
+
+def from_code(code):
+    z = code.astype(jnp.float32)
+    root = jnp.maximum(jnp.abs(z), CODE_FLOOR)
+    root = root * lax.rsqrt(root)
+    root = root * lax.rsqrt(root) * (1.0 / CODE_SCALE)
+    return jnp.where(z > 0.0, root, jnp.where(z < 0.0, -root, 0.0))
+
+
 def forward_kernel(
     rows_in, cols_in, count_in, source, tiles, keep, send, block, acc, rows, cols, count, sems
 ):
@@ -118,16 +133,16 @@
             mine = pl.multiple_of(base + me * own_rows, own_rows)
             other = pl.multiple_of(base + (1 - me) * own_rows, own_rows)
             keep[t * pieces + q] = acc[t, pl.ds(mine, own_rows), :]
-            send[t * pieces + q] = acc[t, pl.ds(other, own_rows), :].astype(send.dtype)
+            send[t * pieces + q] = to_code(acc[t, pl.ds(other, own_rows), :])
 
 
 def add_kernel(keep, received, out):
     other = 1 - lax.axis_index("rep")
-    out[...] = (keep[...] + received[other].astype(jnp.float32)).astype(out.dtype)
+    out[...] = to_code(keep[...] + from_code(received[other]))
 
 
 def dense_kernel(parts, deg, own, pre_self, cotangent, w_neigh, down_self, down_neigh, hidden, d_own, send):
-    agg = jnp.sum(parts[...].astype(jnp.float32), axis=0)
+    agg = jnp.sum(from_code(parts[...]), axis=0)
     degree = deg[...]
     neigh = (agg / degree).astype(jnp.bfloat16)
     pre = pre_self[...] + jnp.dot(neigh, w_neigh[...], preferred_element_type=jnp.float32)
@@ -205,17 +220,27 @@
         send[j] = share
 
 
-def finish_kernel(gathered, parts, hidden_in, d_own_in, hidden, d_src, d_own, grad_self, grad_neigh):
+def finish_kernel(
+    gathered, parts, hidden_in, d_own_in,
+    hidden, d_src, d_own, grad_self, grad_neigh, grads, src, sems,
+):
+    copies = [pltpu.make_async_copy(x, y.at[0], sems.at[i]) for i, (x, y) in enumerate(((hidden_in, hidden), (d_own_in, d_own)))]
+    for copy in copies:
+        copy.start()
     ncol, n, feat = gathered.shape
     per = feat // n
-    for j in range(ncol):
-        lane, row = divmod(j, 2 * per)
-        which, row = divmod(row, per)
-        out = (grad_self, grad_neigh)[which]
-        out[row * n : (row + 1) * n, lane * feat : (lane + 1) * feat] = gathered[j].astype(jnp.float32)
-    d_src[0] = jnp.sum(parts[:, : d_src.shape[1]].astype(jnp.float32), axis=0).astype(d_src.dtype)
-    hidden[0] = hidden_in[...]
-    d_own[0] = d_own_in[...]
+    for which, out in enumerate((grad_self, grad_neigh)):
+        for lane in range(ncol // (2 * per)):
+            for row in range(per):
+                j = (2 * lane + which) * per + row
+                grads[which, row * n : (row + 1) * n, lane * feat : (lane + 1) * feat] = gathered[j].astype(jnp.float32)
+        copies.append(pltpu.make_async_copy(grads.at[which], out, sems.at[2 + which]))
+        copies[-1].start()
+    src[...] = jnp.sum(parts[:, : src.shape[0]].astype(jnp.float32), axis=0).astype(src.dtype)
+    copies.append(pltpu.make_async_copy(src, d_src.at[0], sems.at[4]))
+    copies[-1].start()
+    for copy in copies:
+        copy.wait()
 
 
 def exchange(x, axis):
@@ -339,6 +364,12 @@
             shape((feat, hid), f32),
         ),
         (exchange(send, "col"), parts, hidden, d_x_dst),
+        out_specs=(HBM,) * 5,
+        scratch=(
+            pltpu.VMEM((2, feat, hid), f32),
+            pltpu.VMEM((own_src, feat), bf16),
+            pltpu.SemaphoreType.DMA((5,)),
+        ),
     )
 
 

time: 119 us -> 120 us (level)
  no operation moved by 1% of the time
where the time goes in v5:
time: 120 us; the launch traced here: 119 us
  blocking collectives  91.3 us (76%)
  starting transfers between devices  10.1 us (8%)
  Pallas kernels  8.44 us (7%)
  waiting for transfers between devices  4.96 us (4%)
  local copies, waits for them, and re-layouts  2.46 us (2%)
  between operations  1.36 us (1%)
    all_to_all x4, blocking collectives, exchange(): return lax.all_to_all(x, axis, split_axis=0, concat_axis=0, tiled=True)  76.7 us
    all_to_all x1, starting transfers between devices, exchange(): return lax.all_to_all(x, axis, split_axis=0, concat_axis=0, tiled=True)  10.1 us
    pallas_call x10, Pallas kernels, call(): pl.pallas_call(kernel, out_shape=out_shape, in_specs=in_specs or [VMEM] *...  8.44 us
    all_gather x2, blocking collectives, on_device(): received = lax.all_gather(send, 'rep', axis=0)  5.42 us
    all_gather x1, blocking collectives, on_device(): gathered = lax.all_gather(dagg, 'rep', axis=0)  5.09 us
    all_to_all x1, waiting for transfers between devices, exchange(): return lax.all_to_all(x, axis, split_axis=0, concat_axis=0, tiled=True)  4.96 us
    all_gather x1, blocking collectives, on_device(): source = lax.all_gather(source, 'rep', axis=0)  4.07 us
    unnamed x16, local copies, waits for them, and re-layouts  2.46 us
  transfers between devices with their start and end apart: 1, of which 1 were waited for; matrix products, arithmetic and copies ran while one was open for 0% of the time, Pallas kernels for 2%

profile of v5, /device:TPU:1, one launch (start us, length us, event | category | flops | bytes accessed | tf_op | source)
XLA Modules:
  0.0 118.6 jit_solution(1386525048334672463)
XLA Ops:
  0.6 1.5 %shard_map.138 = bf16[8,128,128]{2,1,0:T(8,128)(2,1)} custom-call(bf16[1,128,128]{2,1,0:T(8,128)(2,1)} %x.1), custom_call_target="tpu_custom_call" | custom-call | tf_op jit(solution)/shard_map/pallas_call | solution.py:22
  2.1 10.1 %all-to-all-start = ((bf16[8,128,128]{2,1,0:T(8,128)(2,1)}), bf16[8,128,128]{2,1,0:T(8,128)(2,1)}, u32[]{:S(2)}, u32[]{:S(2)}) async-start(bf16[8,128,128]{2,1,0:T(8,128)(2,1)} %shard_map.138), calls=%async_computation | async-start | bytes 524288 | tf_op jit(solution)/shard_map/all_to_all | solution.py:247
  12.9 2.2 %shard_map.137 = (s32[24]{0:T(128)S(1)}, s32[24]{0:T(128)S(1)}, s32[8,128]{1,0:T(8,128)S(1)}, bf16[24,256,256]{2,1,0:T(8,128)(2,1)S(1)}, f32[32,1]{1,0:T(8,128)S...) custom-call(s32[24]{0:T(128)} %bitcast.12, ...), custom_call_target="tpu_custom_call" | custom-call | bytes 6291456 | tf_op jit(solution)/shard_map/pallas_call | solution.py:22
  15.1 0.0 copy-start
  15.1 0.6 copy-done
  15.8 0.0 copy-start.2
  15.8 0.6 copy-done.2
  16.4 0.0 copy-start.4
  16.4 0.6 copy-done.4
  17.0 0.0 copy-start.6
  17.0 0.6 copy-done.6
  17.6 5.0 %all-to-all-done = bf16[8,128,128]{2,1,0:T(8,128)(2,1)} async-done(((bf16[8,128,128]{2,1,0:T(8,128)(2,1)}), bf16[8,128,128]{2,1,0:T(8,128)(2,1)}, u32[]{:S(2)}, u32[]{:S(2)}) %all-to-all-start) | async-done | bytes 262176 | tf_op jit(solution)/shard_map/all_to_all | solution.py:247
  22.5 4.1 %all-gather = bf16[16,128,128]{2,1,0:T(8,128)(2,1)S(1)} all-gather(bf16[8,128,128]{2,1,0:T(8,128)(2,1)} %all-to-all-done), channel_id=2, replica_groups=mesh['row'=8,'col'=32,'rep'=2] {'rep'}, dimensions={0}, use_global_device_ids=true | all-gather | bytes 786432 | tf_op jit(solution)/shard_map/all_gather | solution.py:302
  26.6 0.0 copy-start.1
  26.6 0.0 copy-start.3
  26.6 0.0 copy-start.5
  26.6 0.0 copy-start.7
  26.6 1.3 %shard_map.139 = (f32[32,32,128]{2,1,0:T(8,128)S(1)}, bf16[32,32,128]{2,1,0:T(8,128)(2,1)S(1)}) custom-call(s32[24]{0:T(128)S(1)} %get-tuple-element.25.rows_in, s32[24]{0:T(128)S(1)} %get-tuple-element.26.cols_in, s32[8,128]{1,0:T(8,128)S(1)} %get-tuple-element.27.count_in, bf16[2,8,128,128]{3,2,1,0:T(8,128)(2,1)S(1)} %bitcast.9, ...), custom_call_target="tpu_custom_call" | custom-call | flops 402653184 | bytes 3145728 | tf_op jit(solution)/shard_map/pallas_call | solution.py:22
  27.9 2.7 %all-gather.1 = bf16[64,32,128]{2,1,0:T(8,128)(2,1)S(1)} all-gather(bf16[32,32,128]{2,1,0:T(8,128)(2,1)S(1)} %get-tuple-element.30), channel_id=3, replica_groups=mesh['row'=8,'col'=32,'rep'=2] {'rep'}, dimensions={0}, use_global_device_ids=true | all-gather | bytes 786432 | tf_op jit(solution)/shard_map/all_gather | solution.py:315
  30.6 0.3 shard_map.140
  31.0 25.2 %all_to_all.25.parts = bf16[32,32,128]{2,1,0:T(8,128)(2,1)S(1)} all-to-all(bf16[32,32,128]{2,1,0:T(8,128)(2,1)S(1)} %shard_map.140), channel_id=1, replica_groups=mesh['row'=8,'col'=32,'rep'=2] {'col'}, dimensions={0} | all-to-all | bytes 524288 | tf_op jit(solution)/shard_map/all_to_all | solution.py:247
  56.2 0.0 copy-done.1
  56.2 0.0 copy-done.3
  56.2 0.0 copy-done.5
  56.2 0.0 copy-done.7
  56.2 0.7 shard_map.141
  56.9 19.4 %all_to_all.26.both = bf16[32,64,128]{2,1,0:T(8,128)(2,1)S(1)} all-to-all(bf16[32,64,128]{2,1,0:T(8,128)(2,1)S(1)} %get-tuple-element.38), channel_id=1, replica_groups=mesh['row'=8,'col'=32,'rep'=2] {'col'}, dimensions={0} | all-to-all | bytes 1048576 | tf_op jit(solution)/shard_map/all_to_all | solution.py:247
  76.3 0.1 shard_map.142
  76.3 5.1 %all-gather.2 = bf16[64,32,128]{2,1,0:T(8,128)(2,1)S(1)} all-gather(bf16[32,32,128]{2,1,0:T(8,128)(2,1)S(1)} %get-tuple-element.39), channel_id=4, replica_groups=mesh['row'=8,'col'=32,'rep'=2] {'rep'}, dimensions={0}, use_global_device_ids=true | all-gather | bytes 786432 | tf_op jit(solution)/shard_map/all_gather | solution.py:336
  81.4 1.4 %shard_map.143 = (f32[8,128,128]{2,1,0:T(8,128)S(1)}, bf16[1056,128]{1,0:T(8,128)(2,1)S(1)}) custom-call(s32[24]{0:T(128)S(1)} %get-tuple-element.25.rows_in, s32[24]{0:T(128)S(1)} %get-tuple-element.26.cols_in, s32[8,128]{1,0:T(8,128)S(1)} %get-tuple-element.27.count_in, bf16[2,32,32,128]{3,2,1,0:T(8,128)(2,1)S(1)} %bitcast.8, ...), custom_call_target="tpu_custom_call" | custom-call | flops 402653184 | bytes 3145728 | tf_op jit(solution)/shard_map/pallas_call | solution.py:22
  82.9 2.7 %all-gather.3 = bf16[2112,128]{1,0:T(8,128)(2,1)S(1)} all-gather(bf16[1056,128]{1,0:T(8,128)(2,1)S(1)} %get-tuple-element.42), channel_id=5, replica_groups=mesh['row'=8,'col'=32,'rep'=2] {'rep'}, dimensions={0}, use_global_device_ids=true | all-gather | bytes 811008 | tf_op jit(solution)/shard_map/all_gather | solution.py:349
  85.6 0.1 shard_map.144
  85.6 13.9 %all_to_all.27.parts = bf16[8,160,128]{2,1,0:T(8,128)(2,1)S(1)} all-to-all(bf16[8,160,128]{2,1,0:T(8,128)(2,1)S(1)} %shard_map.144), channel_id=1, replica_groups=mesh['row'=8,'col'=32,'rep'=2] {'row'}, dimensions={0} | all-to-all | bytes 655360 | tf_op jit(solution)/shard_map/all_to_all | solution.py:247
  99.6 18.2 %all_to_all.28.gathered = bf16[32,32,128]{2,1,0:T(8,128)(2,1)S(1)} all-to-all(bf16[32,32,128]{2,1,0:T(8,128)(2,1)S(1)} %shard_map.145), channel_id=1, replica_groups=mesh['row'=8,'col'=32,'rep'=2] {'col'}, dimensions={0} | all-to-all | bytes 524288 | tf_op jit(solution)/shard_map/all_to_all | solution.py:247
  117.8 0.9 shard_map.146
  (1 shorter events, 0.0 us)
Async XLA Ops:
  2.1 20.4 %all-to-all-start = ((bf16[8,128,128]{2,1,0:T(8,128)(2,1)}), bf16[8,128,128]{2,1,0:T(8,128)(2,1)}, u32[]{:S(2)}, u32[]{:S(2)}) async-start(bf16[8,128,128]{2,1,0:T(8,128)(2,1)} %shard_map.138), calls=%async_computation | async-start | bytes 524288 | tf_op jit(solution)/shard_map/all_to_all | solution.py:247
  15.1 0.6 copy-start
  15.8 0.6 copy-start.2
  16.4 0.6 copy-start.4
  17.0 0.6 copy-start.6
  26.6 29.6 %copy-start.1 = (f32[32,512]{1,0:T(8,128)S(1)}, f32[32,512]{1,0:T(8,128)}, u32[]{:S(2)}) copy-start(f32[32,512]{1,0:T(8,128)} %copy-done) | copy-start | bytes 196612
  26.6 29.6 %copy-start.3 = (bf16[128,32]{1,0:T(8,128)(2,1)S(1)}, bf16[128,32]{1,0:T(8,128)(2,1)}, u32[]{:S(2)}) copy-start(bf16[128,32]{1,0:T(8,128)(2,1)} %copy-done.2) | copy-start | bytes 24580
  26.6 29.6 %copy-start.5 = (bf16[1,32,512]{2,1,0:T(8,128)(2,1)S(1)}, bf16[1,32,512]{2,1,0:T(8,128)(2,1)}, u32[]{:S(2)}) copy-start(bf16[1,32,512]{2,1,0:T(8,128)(2,1)} %copy-done.4) | copy-start | bytes 98308
  26.6 29.6 %copy-start.7 = (f32[32,1]{1,0:T(8,128)S(1)}, f32[32,1]{1,0:T(8,128)}, u32[]{:S(2)}) copy-start(f32[32,1]{1,0:T(8,128)} %copy-done.6) | copy-start | bytes 388

commit v6 on v5

--- a/solution.py
+++ b/solution.py
@@ -49,8 +49,9 @@
     copy = pltpu.make_async_copy(x, held, sem)
     copy.start()
     copy.wait()
+    scaled = held[0] * jnp.asarray(CODE_SCALE, held.dtype)
     for r in range(out.shape[0]):
-        out[r] = held[0]
+        out[r] = scaled
 
 
 def fetch_kernel(
@@ -93,16 +94,15 @@
 
 
 def to_code(x):
-    y = x * CODE_SCALE
-    return (y * jnp.abs(y) * (y * y)).astype(jnp.bfloat16)
+    return (x * jnp.abs(x) * (x * x)).astype(jnp.bfloat16)
 
 
 def from_code(code):
     z = code.astype(jnp.float32)
     root = jnp.maximum(jnp.abs(z), CODE_FLOOR)
     root = root * lax.rsqrt(root)
-    root = root * lax.rsqrt(root) * (1.0 / CODE_SCALE)
-    return jnp.where(z > 0.0, root, jnp.where(z < 0.0, -root, 0.0))
+    root = root * lax.rsqrt(root)
+    return jnp.where(z < 0.0, -root, root)
 
 
 def forward_kernel(
@@ -142,7 +142,7 @@
 
 
 def dense_kernel(parts, deg, own, pre_self, cotangent, w_neigh, down_self, down_neigh, hidden, d_own, send):
-    agg = jnp.sum(from_code(parts[...]), axis=0)
+    agg = jnp.sum(from_code(parts[...]), axis=0) * (1.0 / CODE_SCALE)
     degree = deg[...]
     neigh = (agg / degree).astype(jnp.bfloat16)
     pre = pre_self[...] + jnp.dot(neigh, w_neigh[...], preferred_element_type=jnp.float32)

time: 120 us -> 119 us (level)
    all_to_all x4, blocking collectives: 76.7 us -> 78.6 us  [exchange(): return lax.all_to_all(x, axis, split_axis=0, concat_axis=0, tiled=True)]
where the time goes in v6:
time: 119 us
  blocking collectives  92.1 us (77%)
  starting transfers between devices  10.1 us (8%)
  Pallas kernels  7.58 us (6%)
  waiting for transfers between devices  4.96 us (4%)
  local copies, waits for them, and re-layouts  2.46 us (2%)
  between operations  1.37 us (1%)
    all_to_all x4, blocking collectives, exchange(): return lax.all_to_all(x, axis, split_axis=0, concat_axis=0, tiled=True)  78.6 us
    all_to_all x1, starting transfers between devices, exchange(): return lax.all_to_all(x, axis, split_axis=0, concat_axis=0, tiled=True)  10.1 us
    pallas_call x10, Pallas kernels, call(): pl.pallas_call(kernel, out_shape=out_shape, in_specs=in_specs or [VMEM] *...  7.58 us
    all_gather x1, blocking collectives, on_device(): gathered = lax.all_gather(dagg, 'rep', axis=0)  5.09 us
    all_to_all x1, waiting for transfers between devices, exchange(): return lax.all_to_all(x, axis, split_axis=0, concat_axis=0, tiled=True)  4.96 us
    all_gather x2, blocking collectives, on_device(): received = lax.all_gather(send, 'rep', axis=0)  4.38 us
    all_gather x1, blocking collectives, on_device(): source = lax.all_gather(source, 'rep', axis=0)  4.07 us
    unnamed x16, local copies, waits for them, and re-layouts  2.46 us
  transfers between devices with their start and end apart: 1, of which 1 were waited for; matrix products, arithmetic and copies ran while one was open for 0% of the time, Pallas kernels for 2%

profile of v6, /device:TPU:1, one launch (start us, length us, event | category | flops | bytes accessed | tf_op | source)
XLA Modules:
  0.0 118.6 jit_solution(10887581823409893227)
XLA Ops:
  0.6 1.5 %shard_map.138 = bf16[8,128,128]{2,1,0:T(8,128)(2,1)} custom-call(bf16[1,128,128]{2,1,0:T(8,128)(2,1)} %x.1), custom_call_target="tpu_custom_call" | custom-call | tf_op jit(solution)/shard_map/pallas_call | solution.py:22
  2.1 10.1 %all-to-all-start = ((bf16[8,128,128]{2,1,0:T(8,128)(2,1)}), bf16[8,128,128]{2,1,0:T(8,128)(2,1)}, u32[]{:S(2)}, u32[]{:S(2)}) async-start(bf16[8,128,128]{2,1,0:T(8,128)(2,1)} %shard_map.138), calls=%async_computation | async-start | bytes 524288 | tf_op jit(solution)/shard_map/all_to_all | solution.py:247
  12.9 2.2 %shard_map.137 = (s32[24]{0:T(128)S(1)}, s32[24]{0:T(128)S(1)}, s32[8,128]{1,0:T(8,128)S(1)}, bf16[24,256,256]{2,1,0:T(8,128)(2,1)S(1)}, f32[32,1]{1,0:T(8,128)S...) custom-call(s32[24]{0:T(128)} %bitcast.12, ...), custom_call_target="tpu_custom_call" | custom-call | bytes 6291456 | tf_op jit(solution)/shard_map/pallas_call | solution.py:22
  15.1 0.0 copy-start
  15.1 0.6 copy-done
  15.7 0.0 copy-start.2
  15.7 0.6 copy-done.2
  16.4 0.0 copy-start.4
  16.4 0.6 copy-done.4
  17.0 0.0 copy-start.6
  17.0 0.6 copy-done.6
  17.6 5.0 %all-to-all-done = bf16[8,128,128]{2,1,0:T(8,128)(2,1)} async-done(((bf16[8,128,128]{2,1,0:T(8,128)(2,1)}), bf16[8,128,128]{2,1,0:T(8,128)(2,1)}, u32[]{:S(2)}, u32[]{:S(2)}) %all-to-all-start) | async-done | bytes 262176 | tf_op jit(solution)/shard_map/all_to_all | solution.py:247
  22.5 4.1 %all-gather = bf16[16,128,128]{2,1,0:T(8,128)(2,1)S(1)} all-gather(bf16[8,128,128]{2,1,0:T(8,128)(2,1)} %all-to-all-done), channel_id=2, replica_groups=mesh['row'=8,'col'=32,'rep'=2] {'rep'}, dimensions={0}, use_global_device_ids=true | all-gather | bytes 786432 | tf_op jit(solution)/shard_map/all_gather | solution.py:302
  26.6 0.0 copy-start.1
  26.6 0.0 copy-start.3
  26.6 0.0 copy-start.5
  26.6 0.0 copy-start.7
  26.6 0.9 shard_map.139
  27.5 2.2 %all-gather.1 = bf16[64,32,128]{2,1,0:T(8,128)(2,1)S(1)} all-gather(bf16[32,32,128]{2,1,0:T(8,128)(2,1)S(1)} %get-tuple-element.30), channel_id=3, replica_groups=mesh['row'=8,'col'=32,'rep'=2] {'rep'}, dimensions={0}, use_global_device_ids=true | all-gather | bytes 786432 | tf_op jit(solution)/shard_map/all_gather | solution.py:315
  29.7 0.3 shard_map.140
  30.0 25.8 %all_to_all.25.parts = bf16[32,32,128]{2,1,0:T(8,128)(2,1)S(1)} all-to-all(bf16[32,32,128]{2,1,0:T(8,128)(2,1)S(1)} %shard_map.140), channel_id=1, replica_groups=mesh['row'=8,'col'=32,'rep'=2] {'col'}, dimensions={0} | all-to-all | bytes 524288 | tf_op jit(solution)/shard_map/all_to_all | solution.py:247
  55.8 0.0 copy-done.1
  55.8 0.0 copy-done.3
  55.8 0.0 copy-done.5
  55.8 0.0 copy-done.7
  55.8 0.6 shard_map.141
  56.4 19.5 %all_to_all.26.both = bf16[32,64,128]{2,1,0:T(8,128)(2,1)S(1)} all-to-all(bf16[32,64,128]{2,1,0:T(8,128)(2,1)S(1)} %get-tuple-element.38), channel_id=1, replica_groups=mesh['row'=8,'col'=32,'rep'=2] {'col'}, dimensions={0} | all-to-all | bytes 1048576 | tf_op jit(solution)/shard_map/all_to_all | solution.py:247
  76.0 0.1 shard_map.142
  76.0 5.1 %all-gather.2 = bf16[64,32,128]{2,1,0:T(8,128)(2,1)S(1)} all-gather(bf16[32,32,128]{2,1,0:T(8,128)(2,1)S(1)} %get-tuple-element.39), channel_id=4, replica_groups=mesh['row'=8,'col'=32,'rep'=2] {'rep'}, dimensions={0}, use_global_device_ids=true | all-gather | bytes 786432 | tf_op jit(solution)/shard_map/all_gather | solution.py:336
  81.1 1.1 shard_map.143
  82.2 2.2 %all-gather.3 = bf16[2112,128]{1,0:T(8,128)(2,1)S(1)} all-gather(bf16[1056,128]{1,0:T(8,128)(2,1)S(1)} %get-tuple-element.42), channel_id=5, replica_groups=mesh['row'=8,'col'=32,'rep'=2] {'rep'}, dimensions={0}, use_global_device_ids=true | all-gather | bytes 811008 | tf_op jit(solution)/shard_map/all_gather | solution.py:349
  84.4 0.1 shard_map.144
  84.5 14.2 %all_to_all.27.parts = bf16[8,160,128]{2,1,0:T(8,128)(2,1)S(1)} all-to-all(bf16[8,160,128]{2,1,0:T(8,128)(2,1)S(1)} %shard_map.144), channel_id=1, replica_groups=mesh['row'=8,'col'=32,'rep'=2] {'row'}, dimensions={0} | all-to-all | bytes 655360 | tf_op jit(solution)/shard_map/all_to_all | solution.py:247
  98.7 19.0 %all_to_all.28.gathered = bf16[32,32,128]{2,1,0:T(8,128)(2,1)S(1)} all-to-all(bf16[32,32,128]{2,1,0:T(8,128)(2,1)S(1)} %shard_map.145), channel_id=1, replica_groups=mesh['row'=8,'col'=32,'rep'=2] {'col'}, dimensions={0} | all-to-all | bytes 524288 | tf_op jit(solution)/shard_map/all_to_all | solution.py:247
  117.7 0.9 shard_map.146
  (1 shorter events, 0.0 us)
Async XLA Ops:
  2.1 20.4 %all-to-all-start = ((bf16[8,128,128]{2,1,0:T(8,128)(2,1)}), bf16[8,128,128]{2,1,0:T(8,128)(2,1)}, u32[]{:S(2)}, u32[]{:S(2)}) async-start(bf16[8,128,128]{2,1,0:T(8,128)(2,1)} %shard_map.138), calls=%async_computation | async-start | bytes 524288 | tf_op jit(solution)/shard_map/all_to_all | solution.py:247
  15.1 0.6 copy-start
  15.7 0.6 copy-start.2
  16.4 0.6 copy-start.4
  17.0 0.6 copy-start.6
  26.6 29.2 %copy-start.1 = (f32[32,512]{1,0:T(8,128)S(1)}, f32[32,512]{1,0:T(8,128)}, u32[]{:S(2)}) copy-start(f32[32,512]{1,0:T(8,128)} %copy-done) | copy-start | bytes 196612
  26.6 29.2 %copy-start.3 = (bf16[128,32]{1,0:T(8,128)(2,1)S(1)}, bf16[128,32]{1,0:T(8,128)(2,1)}, u32[]{:S(2)}) copy-start(bf16[128,32]{1,0:T(8,128)(2,1)} %copy-done.2) | copy-start | bytes 24580
  26.6 29.2 %copy-start.5 = (bf16[1,32,512]{2,1,0:T(8,128)(2,1)S(1)}, bf16[1,32,512]{2,1,0:T(8,128)(2,1)}, u32[]{:S(2)}) copy-start(bf16[1,32,512]{2,1,0:T(8,128)(2,1)} %copy-done.4) | copy-start | bytes 98308
  26.6 29.2 %copy-start.7 = (f32[32,1]{1,0:T(8,128)S(1)}, f32[32,1]{1,0:T(8,128)}, u32[]{:S(2)}) copy-start(f32[32,1]{1,0:T(8,128)} %copy-done.6) | copy-start | bytes 388

commit v7 on v6

--- a/solution.py
+++ b/solution.py
@@ -30,28 +30,35 @@
     )(*operands)
 
 
-def each_live(count, step, group=8):
-    def many(g, carry):
-        for u in range(group):
-            step(g * group + u)
-        return carry
-
-    def one(k, carry):
-        step(k)
-        return carry
-
-    groups = count // group
-    lax.fori_loop(0, groups, many, 0)
-    lax.fori_loop(groups * group, count, one, 0)
-
-
-def spread_kernel(x, out, held, sem):
-    copy = pltpu.make_async_copy(x, held, sem)
-    copy.start()
-    copy.wait()
-    scaled = held[0] * jnp.asarray(CODE_SCALE, held.dtype)
-    for r in range(out.shape[0]):
-        out[r] = scaled
+def each_live(count, step, groups=(12, 4, 1)):
+    done = 0
+    for group in groups:
+
+        def many(g, carry, group=group, done=done):
+            for u in range(group):
+                step(done + g * group + u)
+            return carry
+
+        times = (count - done) // group
+        lax.fori_loop(0, times, many, 0)
+        done = done + times * group
+
+
+def spread_kernel(x, out, held, in_sems, out_sems):
+    half = x.shape[1] // 2
+    spans = [slice(i * half, (i + 1) * half) for i in range(2)]
+    reads = [pltpu.make_async_copy(x.at[0, rows], held.at[rows], in_sems.at[i]) for i, rows in enumerate(spans)]
+    for copy in reads:
+        copy.start()
+    writes = []
+    for i, (copy, rows) in enumerate(zip(reads, spans)):
+        copy.wait()
+        held[rows] = held[rows] * jnp.asarray(CODE_SCALE, held.dtype)
+        for r in range(out.shape[0]):
+            writes.append(pltpu.make_async_copy(held.at[rows], out.at[r, rows], out_sems.at[i, r]))
+            writes[-1].start()
+    for copy in writes:
+        copy.wait()
 
 
 def fetch_kernel(
@@ -141,7 +148,7 @@
     out[...] = to_code(keep[...] + from_code(received[other]))
 
 
-def dense_kernel(parts, deg, own, pre_self, cotangent, w_neigh, down_self, down_neigh, hidden, d_own, send):
+def dense_kernel(parts, deg, own, pre_self, cotangent, w_neigh, down_self, down_neigh, hidden, d_own, dagg_out, w_keep, w_send, grads):
     agg = jnp.sum(from_code(parts[...]), axis=0) * (1.0 / CODE_SCALE)
     degree = deg[...]
     neigh = (agg / degree).astype(jnp.bfloat16)
@@ -154,35 +161,50 @@
     dpre = (cotangent[0].astype(jnp.float32) * slope).astype(jnp.bfloat16)
     d_own[...] = jnp.dot(dpre, down_self[...], preferred_element_type=jnp.float32).astype(d_own.dtype)
     dagg = jnp.dot(dpre, down_neigh[...], preferred_element_type=jnp.float32) / degree
-    dagg = dagg.astype(send.dtype)
-    grads = [
-        jnp.dot(lhs, dpre, preferred_element_type=jnp.float32).astype(send.dtype) for lhs in (own[...], neigh.T)
-    ]
+    dagg_out[...] = dagg.astype(dagg_out.dtype)
+    for which, lhs in enumerate((own[...], neigh.T)):
+        grads[which] = jnp.dot(lhs, dpre, preferred_element_type=jnp.float32)
     feat, n = own.shape
     per = feat // n
-    for j in range(send.shape[0]):
+    share = w_keep.shape[1]
+    me = lax.axis_index("rep")
+    mine, other = (pl.multiple_of(c * share, share) for c in (me, 1 - me))
+    for j in range(w_keep.shape[0]):
         lane, row = divmod(j, 2 * per)
         which, row = divmod(row, per)
-        send[j, :n] = dagg
-        send[j, n:] = grads[which][row * n : (row + 1) * n, lane * feat : (lane + 1) * feat]
-
-
-def split_kernel(both, dagg, share):
-    n = dagg.shape[1]
-    dagg[...] = both[:, :n]
-    share[...] = jnp.sum(both[:, n:].astype(jnp.float32), axis=0)
+        lanes = slice(lane * feat, (lane + 1) * feat)
+        w_keep[j] = grads[which, pl.ds(row * n + mine, share), lanes]
+        w_send[j] = grads[which, pl.ds(row * n + other, share), lanes].astype(w_send.dtype)
+
+
+def pack_kernel(dagg, w_keep, received, send):
+    n = dagg.shape[0]
+    other = 1 - lax.axis_index("rep")
+    for j in range(send.shape[0]):
+        send[j, :n] = dagg[...]
+    send[:, n:] = (w_keep[...] + received[other].astype(jnp.float32)).astype(send.dtype)
+
+
+def split_kernel(both, out):
+    ncol, wide, _ = both.shape
+    n = wide * 2 // 3
+    for j in range(ncol):
+        out[j * n : (j + 1) * n] = both[j, :n]
+    out[ncol * n :] = jnp.sum(both[:, n:].astype(jnp.float32), axis=0).astype(out.dtype)
 
 
 def backward_kernel(
-    rows_in, cols_in, count_in, gathered, tiles, share, keep, send, block, acc, rows, cols, count, sems
+    rows_in, cols_in, count_in, gathered, tiles, keep, send, block, acc, rows, cols, count, sems
 ):
     wait = load_scalars((rows_in, cols_in, count_in), (rows, cols, count), sems)
-    nrep, ncol, own_rows, feat = gathered.shape
+    nrep, _, feat = gathered.shape
     tile = tiles.shape[-1]
-    pieces = tile // (own_rows * nrep)
+    part = tile // nrep
+    n = (gathered.shape[1] - block.shape[0] * part) * nrep
+    pieces = part // n
     for t in range(block.shape[0]):
         upstream = jnp.concatenate(
-            [gathered[c, t * pieces + q] for q in range(pieces) for c in range(nrep)], axis=0
+            [gathered[c, (t * pieces + q) * n : (t * pieces + q + 1) * n] for q in range(pieces) for c in range(nrep)], axis=0
         )
         block[t] = upstream.T
     acc[...] = jnp.zeros_like(acc)
@@ -196,21 +218,20 @@
             acc[where, c] += part[:, c * feat : (c + 1) * feat]
 
     each_live(count[0, 0], step)
-    n = keep.shape[1]
     for t in range(acc.shape[0]):
         keep[t] = acc[t, me].T
-        send[t * n : (t + 1) * n] = acc[t, 1 - me].T.astype(send.dtype)
-    send[acc.shape[0] * n :] = share[...].astype(send.dtype)
-
-
-def merge_kernel(keep, received, share, out):
+        send[t] = acc[t, 1 - me].T.astype(send.dtype)
+
+
+def merge_kernel(keep, received, gathered, out):
     other = 1 - lax.axis_index("rep")
     nrow, n, _ = keep.shape
-    grad = (share[...] + received[other, nrow * n :].astype(jnp.float32)).astype(out.dtype)
+    nrep = gathered.shape[0]
+    share = (out.shape[1] - n) // nrep
     for r in range(nrow):
-        part = received[other, r * n : (r + 1) * n].astype(jnp.float32)
-        out[r, :n] = (keep[r] + part).astype(out.dtype)
-        out[r, n:] = grad
+        out[r, :n] = (keep[r] + received[other, r].astype(jnp.float32)).astype(out.dtype)
+        for c in range(nrep):
+            out[r, n + c * share : n + (c + 1) * share] = gathered[c, gathered.shape[1] - share :]
 
 
 def total_kernel(parts, send):
@@ -269,7 +290,12 @@
         shape((nrow, own_src, feat), bf16),
         (in_hbm(x_src),),
         in_specs=[HBM],
-        scratch=(pltpu.VMEM(x_src.shape, bf16), pltpu.SemaphoreType.DMA),
+        out_specs=HBM,
+        scratch=(
+            pltpu.VMEM((own_src, feat), bf16),
+            pltpu.SemaphoreType.DMA((2,)),
+            pltpu.SemaphoreType.DMA((2, nrow)),
+        ),
     )
     source = exchange(source, "row")
     places = (tile_rows.reshape(-1), tile_cols.reshape(-1))
@@ -319,25 +345,27 @@
         (keep, received),
     )
     parts = exchange(parts, "col")
-    hidden, d_x_dst, send = call(
+    half = own_rows // nrep
+    hidden, d_x_dst, dagg, keep, send = call(
         dense_kernel,
         (
             shape((own_rows, hid), bf16),
             shape((own_rows, feat), bf16),
-            shape((ncol, 2 * own_rows, feat), bf16),
+            shape((own_rows, feat), bf16),
+            shape((ncol, half, feat), f32),
+            shape((ncol, half, feat), bf16),
         ),
         (parts, *held),
-    )
-    dagg, share = call(
-        split_kernel,
-        (shape((ncol, own_rows, feat), bf16), shape((own_rows, feat), f32)),
-        (exchange(send, "col"),),
-    )
-    gathered = lax.all_gather(dagg, "rep", axis=0)
+        scratch=(pltpu.VMEM((2, feat, hid), f32),),
+    )
+    received = lax.all_gather(send, "rep", axis=0)
+    send = call(pack_kernel, shape((ncol, own_rows + half, feat), bf16), (dagg, keep, received))
+    both = call(split_kernel, shape((ncol * own_rows + half, feat), bf16), (exchange(send, "col"),))
+    gathered = lax.all_gather(both, "rep", axis=0)
     keep, send = call(
         backward_kernel,
-        (shape((nrow, own_src, feat), f32), shape((nrow * own_src + own_rows, feat), bf16)),
-        (*scalars, gathered, tiles, share),
+        (shape((nrow, own_src, feat), f32), shape((nrow, own_src, feat), bf16)),
+        (*scalars, gathered, tiles),
         scratch=(
             pltpu.VMEM((row_tiles, feat, tile), bf16),
             pltpu.VMEM((col_tiles, nrep, feat, tile // nrep), f32),
@@ -350,7 +378,7 @@
     merged = call(
         merge_kernel,
         shape((nrow, own_src + own_rows, feat), bf16),
-        (keep, received, share),
+        (keep, received, gathered),
     )
     parts = exchange(merged, "row")
     send = call(total_kernel, shape((ncol, own_rows, feat), bf16), (parts,))

time: 119 us -> 119 us (level)
    all_to_all x4, blocking collectives: 78.6 us -> 74.6 us  [exchange(): return lax.all_to_all(x, axis, split_axis=0, concat_axis=0, tiled=True)]
    all_gather x2 -> x3, blocking collectives: 4.38 us -> 8.35 us  [on_device(): received = lax.all_gather(send, 'rep', axis=0)]
    pallas_call x10 -> x11, Pallas kernels: 7.58 us -> 7.84 us  [call(): pl.pallas_call(kernel, out_shape=out_shape, in_specs=in_specs or [VMEM] *...]
where the time goes in v7:
time: 119 us; the launch traced here: 118 us
  blocking collectives  91.2 us (77%)
  starting transfers between devices  10.1 us (8%)
  Pallas kernels  7.84 us (7%)
  waiting for transfers between devices  4.96 us (4%)
  local copies, waits for them, and re-layouts  2.46 us (2%)
  between operations  1.36 us (1%)
    all_to_all x4, blocking collectives, exchange(): return lax.all_to_all(x, axis, split_axis=0, concat_axis=0, tiled=True)  74.6 us
    all_to_all x1, starting transfers between devices, exchange(): return lax.all_to_all(x, axis, split_axis=0, concat_axis=0, tiled=True)  10.1 us
    all_gather x3, blocking collectives, on_device(): received = lax.all_gather(send, 'rep', axis=0)  8.35 us
    pallas_call x11, Pallas kernels, call(): pl.pallas_call(kernel, out_shape=out_shape, in_specs=in_specs or [VMEM] *...  7.84 us
    all_to_all x1, waiting for transfers between devices, exchange(): return lax.all_to_all(x, axis, split_axis=0, concat_axis=0, tiled=True)  4.96 us
    all_gather x1, blocking collectives, on_device(): gathered = lax.all_gather(both, 'rep', axis=0)  4.22 us
    all_gather x1, blocking collectives, on_device(): source = lax.all_gather(source, 'rep', axis=0)  4.07 us
    unnamed x16, local copies, waits for them, and re-layouts  2.46 us
  transfers between devices with their start and end apart: 1, of which 1 were waited for; matrix products, arithmetic and copies ran while one was open for 0% of the time, Pallas kernels for 2%

profile of v7, /device:TPU:1, one launch (start us, length us, event | category | flops | bytes accessed | tf_op | source)
XLA Modules:
  0.0 117.9 jit_solution(7037393251430236090)
XLA Ops:
  0.6 1.6 %shard_map.138 = bf16[8,128,128]{2,1,0:T(8,128)(2,1)} custom-call(bf16[1,128,128]{2,1,0:T(8,128)(2,1)} %x.1), custom_call_target="tpu_custom_call" | custom-call | tf_op jit(solution)/shard_map/pallas_call | solution.py:22
  2.2 10.1 %all-to-all-start = ((bf16[8,128,128]{2,1,0:T(8,128)(2,1)}), bf16[8,128,128]{2,1,0:T(8,128)(2,1)}, u32[]{:S(2)}, u32[]{:S(2)}) async-start(bf16[8,128,128]{2,1,0:T(8,128)(2,1)} %shard_map.138), calls=%async_computation | async-start | bytes 524288 | tf_op jit(solution)/shard_map/all_to_all | solution.py:268
  13.0 2.2 %shard_map.137 = (s32[24]{0:T(128)S(1)}, s32[24]{0:T(128)S(1)}, s32[8,128]{1,0:T(8,128)S(1)}, bf16[24,256,256]{2,1,0:T(8,128)(2,1)S(1)}, f32[32,1]{1,0:T(8,128)S...) custom-call(s32[24]{0:T(128)} %bitcast.15, ...), custom_call_target="tpu_custom_call" | custom-call | bytes 6291456 | tf_op jit(solution)/shard_map/pallas_call | solution.py:22
  15.2 0.0 copy-start
  15.2 0.6 copy-done
  15.8 0.0 copy-start.2
  15.8 0.6 copy-done.2
  16.4 0.0 copy-start.4
  16.4 0.6 copy-done.4
  17.1 0.0 copy-start.6
  17.1 0.6 copy-done.6
  17.6 5.0 %all-to-all-done = bf16[8,128,128]{2,1,0:T(8,128)(2,1)} async-done(((bf16[8,128,128]{2,1,0:T(8,128)(2,1)}), bf16[8,128,128]{2,1,0:T(8,128)(2,1)}, u32[]{:S(2)}, u32[]{:S(2)}) %all-to-all-start) | async-done | bytes 262176 | tf_op jit(solution)/shard_map/all_to_all | solution.py:268
  22.6 4.1 %all-gather = bf16[16,128,128]{2,1,0:T(8,128)(2,1)S(1)} all-gather(bf16[8,128,128]{2,1,0:T(8,128)(2,1)} %all-to-all-done), channel_id=2, replica_groups=mesh['row'=8,'col'=32,'rep'=2] {'rep'}, dimensions={0}, use_global_device_ids=true | all-gather | bytes 786432 | tf_op jit(solution)/shard_map/all_gather | solution.py:328
  26.7 0.0 copy-start.1
  26.7 0.0 copy-start.3
  26.7 0.0 copy-start.5
  26.7 0.0 copy-start.7
  26.7 0.9 shard_map.139
  27.6 2.4 %all-gather.1 = bf16[64,32,128]{2,1,0:T(8,128)(2,1)S(1)} all-gather(bf16[32,32,128]{2,1,0:T(8,128)(2,1)S(1)} %get-tuple-element.30), channel_id=3, replica_groups=mesh['row'=8,'col'=32,'rep'=2] {'rep'}, dimensions={0}, use_global_device_ids=true | all-gather | bytes 786432 | tf_op jit(solution)/shard_map/all_gather | solution.py:341
  30.0 0.3 shard_map.140
  30.3 25.6 %all_to_all.25.parts = bf16[32,32,128]{2,1,0:T(8,128)(2,1)S(1)} all-to-all(bf16[32,32,128]{2,1,0:T(8,128)(2,1)S(1)} %shard_map.140), channel_id=1, replica_groups=mesh['row'=8,'col'=32,'rep'=2] {'col'}, dimensions={0} | all-to-all | bytes 524288 | tf_op jit(solution)/shard_map/all_to_all | solution.py:268
  55.8 0.0 copy-done.1
  55.8 0.0 copy-done.3
  55.8 0.0 copy-done.5
  55.8 0.0 copy-done.7
  55.8 0.7 shard_map.141
  56.5 3.6 %all-gather.2 = bf16[64,16,128]{2,1,0:T(8,128)(2,1)S(1)} all-gather(bf16[32,16,128]{2,1,0:T(8,128)(2,1)S(1)} %get-tuple-element.40), channel_id=4, replica_groups=mesh['row'=8,'col'=32,'rep'=2] {'rep'}, dimensions={0}, use_global_device_ids=true | all-gather | bytes 393216 | tf_op jit(solution)/shard_map/all_gather | solution.py:361
  60.2 16.7 %all_to_all.26.both = bf16[32,48,128]{2,1,0:T(8,128)(2,1)S(1)} all-to-all(bf16[32,48,128]{2,1,0:T(8,128)(2,1)S(1)} %shard_map.142), channel_id=1, replica_groups=mesh['row'=8,'col'=32,'rep'=2] {'col'}, dimensions={0} | all-to-all | bytes 786432 | tf_op jit(solution)/shard_map/all_to_all | solution.py:268
  77.0 0.1 shard_map.143
  77.0 4.2 %all-gather.3 = bf16[2080,128]{1,0:T(8,128)(2,1)S(1)} all-gather(bf16[1040,128]{1,0:T(8,128)(2,1)S(1)} %shard_map.143), channel_id=5, replica_groups=mesh['row'=8,'col'=32,'rep'=2] {'rep'}, dimensions={0}, use_global_device_ids=true | all-gather | bytes 798720 | tf_op jit(solution)/shard_map/all_gather | solution.py:364
  81.2 1.1 shard_map.144
  82.3 2.4 %all-gather.4 = bf16[16,128,128]{2,1,0:T(8,128)(2,1)S(1)} all-gather(bf16[8,128,128]{2,1,0:T(8,128)(2,1)S(1)} %get-tuple-element.42), channel_id=6, replica_groups=mesh['row'=8,'col'=32,'rep'=2] {'rep'}, dimensions={0}, use_global_device_ids=true | all-gather | bytes 786432 | tf_op jit(solution)/shard_map/all_gather | solution.py:377
  84.7 0.1 shard_map.145
  84.8 13.9 %all_to_all.27.parts = bf16[8,160,128]{2,1,0:T(8,128)(2,1)S(1)} all-to-all(bf16[8,160,128]{2,1,0:T(8,128)(2,1)S(1)} %shard_map.145), channel_id=1, replica_groups=mesh['row'=8,'col'=32,'rep'=2] {'row'}, dimensions={0} | all-to-all | bytes 655360 | tf_op jit(solution)/shard_map/all_to_all | solution.py:268
  98.7 18.4 %all_to_all.28.gathered = bf16[32,32,128]{2,1,0:T(8,128)(2,1)S(1)} all-to-all(bf16[32,32,128]{2,1,0:T(8,128)(2,1)S(1)} %shard_map.146), channel_id=1, replica_groups=mesh['row'=8,'col'=32,'rep'=2] {'col'}, dimensions={0} | all-to-all | bytes 524288 | tf_op jit(solution)/shard_map/all_to_all | solution.py:268
  117.1 0.9 shard_map.147
  (2 shorter events, 0.1 us)
Async XLA Ops:
  2.2 20.4 %all-to-all-start = ((bf16[8,128,128]{2,1,0:T(8,128)(2,1)}), bf16[8,128,128]{2,1,0:T(8,128)(2,1)}, u32[]{:S(2)}, u32[]{:S(2)}) async-start(bf16[8,128,128]{2,1,0:T(8,128)(2,1)} %shard_map.138), calls=%async_computation | async-start | bytes 524288 | tf_op jit(solution)/shard_map/all_to_all | solution.py:268
  15.2 0.6 copy-start
  15.8 0.6 copy-start.2
  16.4 0.6 copy-start.4
  17.1 0.6 copy-start.6
  26.7 29.2 %copy-start.1 = (f32[32,512]{1,0:T(8,128)S(1)}, f32[32,512]{1,0:T(8,128)}, u32[]{:S(2)}) copy-start(f32[32,512]{1,0:T(8,128)} %copy-done) | copy-start | bytes 196612
  26.7 29.2 %copy-start.3 = (bf16[128,32]{1,0:T(8,128)(2,1)S(1)}, bf16[128,32]{1,0:T(8,128)(2,1)}, u32[]{:S(2)}) copy-start(bf16[128,32]{1,0:T(8,128)(2,1)} %copy-done.2) | copy-start | bytes 24580
  26.7 29.2 %copy-start.5 = (bf16[1,32,512]{2,1,0:T(8,128)(2,1)S(1)}, bf16[1,32,512]{2,1,0:T(8,128)(2,1)}, u32[]{:S(2)}) copy-start(bf16[1,32,512]{2,1,0:T(8,128)(2,1)} %copy-done.4) | copy-start | bytes 98308
  26.7 29.2 %copy-start.7 = (f32[32,1]{1,0:T(8,128)S(1)}, f32[32,1]{1,0:T(8,128)}, u32[]{:S(2)}) copy-start(f32[32,1]{1,0:T(8,128)} %copy-done.6) | copy-start | bytes 388

commit v8 on v7

--- a/solution.py
+++ b/solution.py
@@ -30,7 +30,7 @@
     )(*operands)
 
 
-def each_live(count, step, groups=(12, 4, 1)):
+def each_live(count, step, groups=(24, 6, 2, 1)):
     done = 0
     for group in groups:
 

time: 119 us -> 118 us (level)
  blocking collectives: 91.2 us -> 89 us
  Pallas kernels: 7.84 us -> 9.21 us
    all_to_all x4, blocking collectives: 74.6 us -> 72.8 us  [exchange(): return lax.all_to_all(x, axis, split_axis=0, concat_axis=0, tiled=True)]
    pallas_call x11, Pallas kernels: 7.84 us -> 9.21 us  [call(): pl.pallas_call(kernel, out_shape=out_shape, in_specs=in_specs or [VMEM] *...]
where the time goes in v8:
time: 118 us; the launch traced here: 117 us
  blocking collectives  89 us (75%)
  starting transfers between devices  10.1 us (9%)
  Pallas kernels  9.21 us (8%)
  waiting for transfers between devices  4.96 us (4%)
  local copies, waits for them, and re-layouts  2.46 us (2%)
  between operations  1.36 us (1%)
    all_to_all x4, blocking collectives, exchange(): return lax.all_to_all(x, axis, split_axis=0, concat_axis=0, tiled=True)  72.8 us
    all_to_all x1, starting transfers between devices, exchange(): return lax.all_to_all(x, axis, split_axis=0, concat_axis=0, tiled=True)  10.1 us
    pallas_call x11, Pallas kernels, call(): pl.pallas_call(kernel, out_shape=out_shape, in_specs=in_specs or [VMEM] *...  9.21 us
    all_gather x3, blocking collectives, on_device(): received = lax.all_gather(send, 'rep', axis=0)  7.9 us
    all_to_all x1, waiting for transfers between devices, exchange(): return lax.all_to_all(x, axis, split_axis=0, concat_axis=0, tiled=True)  4.96 us
    all_gather x1, blocking collectives, on_device(): gathered = lax.all_gather(both, 'rep', axis=0)  4.22 us
    all_gather x1, blocking collectives, on_device(): source = lax.all_gather(source, 'rep', axis=0)  4.07 us
    unnamed x16, local copies, waits for them, and re-layouts  2.46 us
  transfers between devices with their start and end apart: 1, of which 1 were waited for; matrix products, arithmetic and copies ran while one was open for 0% of the time, Pallas kernels for 2%

profile of v8, /device:TPU:1, one launch (start us, length us, event | category | flops | bytes accessed | tf_op | source)
XLA Modules:
  0.0 117.1 jit_solution(17978701480537974629)
XLA Ops:
  0.6 1.6 %shard_map.138 = bf16[8,128,128]{2,1,0:T(8,128)(2,1)} custom-call(bf16[1,128,128]{2,1,0:T(8,128)(2,1)} %x.1), custom_call_target="tpu_custom_call" | custom-call | tf_op jit(solution)/shard_map/pallas_call | solution.py:22
  2.2 10.1 %all-to-all-start = ((bf16[8,128,128]{2,1,0:T(8,128)(2,1)}), bf16[8,128,128]{2,1,0:T(8,128)(2,1)}, u32[]{:S(2)}, u32[]{:S(2)}) async-start(bf16[8,128,128]{2,1,0:T(8,128)(2,1)} %shard_map.138), calls=%async_computation | async-start | bytes 524288 | tf_op jit(solution)/shard_map/all_to_all | solution.py:268
  13.0 2.2 %shard_map.137 = (s32[24]{0:T(128)S(1)}, s32[24]{0:T(128)S(1)}, s32[8,128]{1,0:T(8,128)S(1)}, bf16[24,256,256]{2,1,0:T(8,128)(2,1)S(1)}, f32[32,1]{1,0:T(8,128)S...) custom-call(s32[24]{0:T(128)} %bitcast.15, ...), custom_call_target="tpu_custom_call" | custom-call | bytes 6291456 | tf_op jit(solution)/shard_map/pallas_call | solution.py:22
  15.2 0.0 copy-start
  15.2 0.6 copy-done
  15.8 0.0 copy-start.2
  15.8 0.6 copy-done.2
  16.4 0.0 copy-start.4
  16.4 0.6 copy-done.4
  17.1 0.0 copy-start.6
  17.1 0.6 copy-done.6
  17.6 5.0 %all-to-all-done = bf16[8,128,128]{2,1,0:T(8,128)(2,1)} async-done(((bf16[8,128,128]{2,1,0:T(8,128)(2,1)}), bf16[8,128,128]{2,1,0:T(8,128)(2,1)}, u32[]{:S(2)}, u32[]{:S(2)}) %all-to-all-start) | async-done | bytes 262176 | tf_op jit(solution)/shard_map/all_to_all | solution.py:268
  22.6 4.1 %all-gather = bf16[16,128,128]{2,1,0:T(8,128)(2,1)S(1)} all-gather(bf16[8,128,128]{2,1,0:T(8,128)(2,1)} %all-to-all-done), channel_id=2, replica_groups=mesh['row'=8,'col'=32,'rep'=2] {'rep'}, dimensions={0}, use_global_device_ids=true | all-gather | bytes 786432 | tf_op jit(solution)/shard_map/all_gather | solution.py:328
  26.7 0.0 copy-start.1
  26.7 0.0 copy-start.3
  26.7 0.0 copy-start.5
  26.7 0.0 copy-start.7
  26.7 1.8 %shard_map.139 = (f32[32,32,128]{2,1,0:T(8,128)S(1)}, bf16[32,32,128]{2,1,0:T(8,128)(2,1)S(1)}) custom-call(s32[24]{0:T(128)S(1)} %get-tuple-element.25.rows_in, s32[24]{0:T(128)S(1)} %get-tuple-element.26.cols_in, s32[8,128]{1,0:T(8,128)S(1)} %get-tuple-element.27.count_in, bf16[2,8,128,128]{3,2,1,0:T(8,128)(2,1)S(1)} %bitcast.10, ...), custom_call_target="tpu_custom_call" | custom-call | flops 402653184 | bytes 3145728 | tf_op jit(solution)/shard_map/pallas_call | solution.py:22
  28.5 2.2 %all-gather.1 = bf16[64,32,128]{2,1,0:T(8,128)(2,1)S(1)} all-gather(bf16[32,32,128]{2,1,0:T(8,128)(2,1)S(1)} %get-tuple-element.30), channel_id=3, replica_groups=mesh['row'=8,'col'=32,'rep'=2] {'rep'}, dimensions={0}, use_global_device_ids=true | all-gather | bytes 786432 | tf_op jit(solution)/shard_map/all_gather | solution.py:341
  30.6 0.3 shard_map.140
  30.9 24.5 %all_to_all.25.parts = bf16[32,32,128]{2,1,0:T(8,128)(2,1)S(1)} all-to-all(bf16[32,32,128]{2,1,0:T(8,128)(2,1)S(1)} %shard_map.140), channel_id=1, replica_groups=mesh['row'=8,'col'=32,'rep'=2] {'col'}, dimensions={0} | all-to-all | bytes 524288 | tf_op jit(solution)/shard_map/all_to_all | solution.py:268
  55.4 0.0 copy-done.1
  55.4 0.0 copy-done.3
  55.4 0.0 copy-done.5
  55.4 0.0 copy-done.7
  55.4 0.7 shard_map.141
  56.1 3.5 %all-gather.2 = bf16[64,16,128]{2,1,0:T(8,128)(2,1)S(1)} all-gather(bf16[32,16,128]{2,1,0:T(8,128)(2,1)S(1)} %get-tuple-element.40), channel_id=4, replica_groups=mesh['row'=8,'col'=32,'rep'=2] {'rep'}, dimensions={0}, use_global_device_ids=true | all-gather | bytes 393216 | tf_op jit(solution)/shard_map/all_gather | solution.py:361
  59.7 16.7 %all_to_all.26.both = bf16[32,48,128]{2,1,0:T(8,128)(2,1)S(1)} all-to-all(bf16[32,48,128]{2,1,0:T(8,128)(2,1)S(1)} %shard_map.142), channel_id=1, replica_groups=mesh['row'=8,'col'=32,'rep'=2] {'col'}, dimensions={0} | all-to-all | bytes 786432 | tf_op jit(solution)/shard_map/all_to_all | solution.py:268
  76.4 0.1 shard_map.143
  76.5 4.2 %all-gather.3 = bf16[2080,128]{1,0:T(8,128)(2,1)S(1)} all-gather(bf16[1040,128]{1,0:T(8,128)(2,1)S(1)} %shard_map.143), channel_id=5, replica_groups=mesh['row'=8,'col'=32,'rep'=2] {'rep'}, dimensions={0}, use_global_device_ids=true | all-gather | bytes 798720 | tf_op jit(solution)/shard_map/all_gather | solution.py:364
  80.7 1.7 %shard_map.144 = (f32[8,128,128]{2,1,0:T(8,128)S(1)}, bf16[8,128,128]{2,1,0:T(8,128)(2,1)S(1)}) custom-call(s32[24]{0:T(128)S(1)} %get-tuple-element.25.rows_in, s32[24]{0:T(128)S(1)} %get-tuple-element.26.cols_in, s32[8,128]{1,0:T(8,128)S(1)} %get-tuple-element.27.count_in, bf16[2,1040,128]{2,1,0:T(8,128)(2,1)S(1)} %bitcast.8, ...), custom_call_target="tpu_custom_call" | custom-call | flops 402653184 | bytes 3145728 | tf_op jit(solution)/shard_map/pallas_call | solution.py:22
  82.4 2.2 %all-gather.4 = bf16[16,128,128]{2,1,0:T(8,128)(2,1)S(1)} all-gather(bf16[8,128,128]{2,1,0:T(8,128)(2,1)S(1)} %get-tuple-element.42), channel_id=6, replica_groups=mesh['row'=8,'col'=32,'rep'=2] {'rep'}, dimensions={0}, use_global_device_ids=true | all-gather | bytes 786432 | tf_op jit(solution)/shard_map/all_gather | solution.py:377
  84.5 0.1 shard_map.145
  84.6 14.0 %all_to_all.27.parts = bf16[8,160,128]{2,1,0:T(8,128)(2,1)S(1)} all-to-all(bf16[8,160,128]{2,1,0:T(8,128)(2,1)S(1)} %shard_map.145), channel_id=1, replica_groups=mesh['row'=8,'col'=32,'rep'=2] {'row'}, dimensions={0} | all-to-all | bytes 655360 | tf_op jit(solution)/shard_map/all_to_all | solution.py:268
  98.7 17.6 %all_to_all.28.gathered = bf16[32,32,128]{2,1,0:T(8,128)(2,1)S(1)} all-to-all(bf16[32,32,128]{2,1,0:T(8,128)(2,1)S(1)} %shard_map.146), channel_id=1, replica_groups=mesh['row'=8,'col'=32,'rep'=2] {'col'}, dimensions={0} | all-to-all | bytes 524288 | tf_op jit(solution)/shard_map/all_to_all | solution.py:268
  116.3 0.9 shard_map.147
  (2 shorter events, 0.1 us)
Async XLA Ops:
  2.2 20.4 %all-to-all-start = ((bf16[8,128,128]{2,1,0:T(8,128)(2,1)}), bf16[8,128,128]{2,1,0:T(8,128)(2,1)}, u32[]{:S(2)}, u32[]{:S(2)}) async-start(bf16[8,128,128]{2,1,0:T(8,128)(2,1)} %shard_map.138), calls=%async_computation | async-start | bytes 524288 | tf_op jit(solution)/shard_map/all_to_all | solution.py:268
  15.2 0.6 copy-start
  15.8 0.6 copy-start.2
  16.4 0.6 copy-start.4
  17.1 0.6 copy-start.6
  26.7 28.7 %copy-start.1 = (f32[32,512]{1,0:T(8,128)S(1)}, f32[32,512]{1,0:T(8,128)}, u32[]{:S(2)}) copy-start(f32[32,512]{1,0:T(8,128)} %copy-done) | copy-start | bytes 196612
  26.7 28.7 %copy-start.3 = (bf16[128,32]{1,0:T(8,128)(2,1)S(1)}, bf16[128,32]{1,0:T(8,128)(2,1)}, u32[]{:S(2)}) copy-start(bf16[128,32]{1,0:T(8,128)(2,1)} %copy-done.2) | copy-start | bytes 24580
  26.7 28.7 %copy-start.5 = (bf16[1,32,512]{2,1,0:T(8,128)(2,1)S(1)}, bf16[1,32,512]{2,1,0:T(8,128)(2,1)}, u32[]{:S(2)}) copy-start(bf16[1,32,512]{2,1,0:T(8,128)(2,1)} %copy-done.4) | copy-start | bytes 98308
  26.7 28.7 %copy-start.7 = (f32[32,1]{1,0:T(8,128)S(1)}, f32[32,1]{1,0:T(8,128)}, u32[]{:S(2)}) copy-start(f32[32,1]{1,0:T(8,128)} %copy-done.6) | copy-start | bytes 388

commit v9 on v8

--- a/solution.py
+++ b/solution.py
@@ -30,7 +30,7 @@
     )(*operands)
 
 
-def each_live(count, step, groups=(24, 6, 2, 1)):
+def each_live(count, step, groups=(12, 4, 2, 1)):
     done = 0
     for group in groups:
 

time: 118 us -> 119 us (level)
  blocking collectives: 89 us -> 90.4 us
where the time goes in v9:
time: 119 us; the launch traced here: 118 us
  blocking collectives  90.4 us (76%)
  starting transfers between devices  10.1 us (8%)
  Pallas kernels  8.28 us (7%)
  waiting for transfers between devices  4.96 us (4%)
  local copies, waits for them, and re-layouts  2.46 us (2%)
  between operations  1.36 us (1%)
    all_to_all x4, blocking collectives, exchange(): return lax.all_to_all(x, axis, split_axis=0, concat_axis=0, tiled=True)  74 us
    all_to_all x1, starting transfers between devices, exchange(): return lax.all_to_all(x, axis, split_axis=0, concat_axis=0, tiled=True)  10.1 us
    pallas_call x11, Pallas kernels, call(): pl.pallas_call(kernel, out_shape=out_shape, in_specs=in_specs or [VMEM] *...  8.28 us
    all_gather x3, blocking collectives, on_device(): received = lax.all_gather(send, 'rep', axis=0)  8.12 us
    all_to_all x1, waiting for transfers between devices, exchange(): return lax.all_to_all(x, axis, split_axis=0, concat_axis=0, tiled=True)  4.96 us
    all_gather x1, blocking collectives, on_device(): gathered = lax.all_gather(both, 'rep', axis=0)  4.22 us
    all_gather x1, blocking collectives, on_device(): source = lax.all_gather(source, 'rep', axis=0)  4.07 us
    unnamed x16, local copies, waits for them, and re-layouts  2.46 us
  transfers between devices with their start and end apart: 1, of which 1 were waited for; matrix products, arithmetic and copies ran while one was open for 0% of the time, Pallas kernels for 2%

profile of v9, /device:TPU:1, one launch (start us, length us, event | category | flops | bytes accessed | tf_op | source)
XLA Modules:
  0.0 117.5 jit_solution(10425453615024197474)
XLA Ops:
  0.6 1.6 %shard_map.138 = bf16[8,128,128]{2,1,0:T(8,128)(2,1)} custom-call(bf16[1,128,128]{2,1,0:T(8,128)(2,1)} %x.1), custom_call_target="tpu_custom_call" | custom-call | tf_op jit(solution)/shard_map/pallas_call | solution.py:22
  2.2 10.1 %all-to-all-start = ((bf16[8,128,128]{2,1,0:T(8,128)(2,1)}), bf16[8,128,128]{2,1,0:T(8,128)(2,1)}, u32[]{:S(2)}, u32[]{:S(2)}) async-start(bf16[8,128,128]{2,1,0:T(8,128)(2,1)} %shard_map.138), calls=%async_computation | async-start | bytes 524288 | tf_op jit(solution)/shard_map/all_to_all | solution.py:268
  13.0 2.2 %shard_map.137 = (s32[24]{0:T(128)S(1)}, s32[24]{0:T(128)S(1)}, s32[8,128]{1,0:T(8,128)S(1)}, bf16[24,256,256]{2,1,0:T(8,128)(2,1)S(1)}, f32[32,1]{1,0:T(8,128)S...) custom-call(s32[24]{0:T(128)} %bitcast.15, ...), custom_call_target="tpu_custom_call" | custom-call | bytes 6291456 | tf_op jit(solution)/shard_map/pallas_call | solution.py:22
  15.2 0.0 copy-start
  15.2 0.6 copy-done
  15.8 0.0 copy-start.2
  15.8 0.6 copy-done.2
  16.4 0.0 copy-start.4
  16.4 0.6 copy-done.4
  17.1 0.0 copy-start.6
  17.1 0.6 copy-done.6
  17.6 5.0 %all-to-all-done = bf16[8,128,128]{2,1,0:T(8,128)(2,1)} async-done(((bf16[8,128,128]{2,1,0:T(8,128)(2,1)}), bf16[8,128,128]{2,1,0:T(8,128)(2,1)}, u32[]{:S(2)}, u32[]{:S(2)}) %all-to-all-start) | async-done | bytes 262176 | tf_op jit(solution)/shard_map/all_to_all | solution.py:268
  22.6 4.1 %all-gather = bf16[16,128,128]{2,1,0:T(8,128)(2,1)S(1)} all-gather(bf16[8,128,128]{2,1,0:T(8,128)(2,1)} %all-to-all-done), channel_id=2, replica_groups=mesh['row'=8,'col'=32,'rep'=2] {'rep'}, dimensions={0}, use_global_device_ids=true | all-gather | bytes 786432 | tf_op jit(solution)/shard_map/all_gather | solution.py:328
  26.7 0.0 copy-start.1
  26.7 0.0 copy-start.3
  26.7 0.0 copy-start.5
  26.7 0.0 copy-start.7
  26.7 1.2 %shard_map.139 = (f32[32,32,128]{2,1,0:T(8,128)S(1)}, bf16[32,32,128]{2,1,0:T(8,128)(2,1)S(1)}) custom-call(s32[24]{0:T(128)S(1)} %get-tuple-element.25.rows_in, s32[24]{0:T(128)S(1)} %get-tuple-element.26.cols_in, s32[8,128]{1,0:T(8,128)S(1)} %get-tuple-element.27.count_in, bf16[2,8,128,128]{3,2,1,0:T(8,128)(2,1)S(1)} %bitcast.10, ...), custom_call_target="tpu_custom_call" | custom-call | flops 402653184 | bytes 3145728 | tf_op jit(solution)/shard_map/pallas_call | solution.py:22
  27.9 2.3 %all-gather.1 = bf16[64,32,128]{2,1,0:T(8,128)(2,1)S(1)} all-gather(bf16[32,32,128]{2,1,0:T(8,128)(2,1)S(1)} %get-tuple-element.30), channel_id=3, replica_groups=mesh['row'=8,'col'=32,'rep'=2] {'rep'}, dimensions={0}, use_global_device_ids=true | all-gather | bytes 786432 | tf_op jit(solution)/shard_map/all_gather | solution.py:341
  30.1 0.3 shard_map.140
  30.4 25.3 %all_to_all.25.parts = bf16[32,32,128]{2,1,0:T(8,128)(2,1)S(1)} all-to-all(bf16[32,32,128]{2,1,0:T(8,128)(2,1)S(1)} %shard_map.140), channel_id=1, replica_groups=mesh['row'=8,'col'=32,'rep'=2] {'col'}, dimensions={0} | all-to-all | bytes 524288 | tf_op jit(solution)/shard_map/all_to_all | solution.py:268
  55.7 0.0 copy-done.1
  55.7 0.0 copy-done.3
  55.7 0.0 copy-done.5
  55.8 0.0 copy-done.7
  55.8 0.7 shard_map.141
  56.4 3.6 %all-gather.2 = bf16[64,16,128]{2,1,0:T(8,128)(2,1)S(1)} all-gather(bf16[32,16,128]{2,1,0:T(8,128)(2,1)S(1)} %get-tuple-element.40), channel_id=4, replica_groups=mesh['row'=8,'col'=32,'rep'=2] {'rep'}, dimensions={0}, use_global_device_ids=true | all-gather | bytes 393216 | tf_op jit(solution)/shard_map/all_gather | solution.py:361
  60.1 16.7 %all_to_all.26.both = bf16[32,48,128]{2,1,0:T(8,128)(2,1)S(1)} all-to-all(bf16[32,48,128]{2,1,0:T(8,128)(2,1)S(1)} %shard_map.142), channel_id=1, replica_groups=mesh['row'=8,'col'=32,'rep'=2] {'col'}, dimensions={0} | all-to-all | bytes 786432 | tf_op jit(solution)/shard_map/all_to_all | solution.py:268
  76.8 0.1 shard_map.143
  76.9 4.2 %all-gather.3 = bf16[2080,128]{1,0:T(8,128)(2,1)S(1)} all-gather(bf16[1040,128]{1,0:T(8,128)(2,1)S(1)} %shard_map.143), channel_id=5, replica_groups=mesh['row'=8,'col'=32,'rep'=2] {'rep'}, dimensions={0}, use_global_device_ids=true | all-gather | bytes 798720 | tf_op jit(solution)/shard_map/all_gather | solution.py:364
  81.1 1.3 %shard_map.144 = (f32[8,128,128]{2,1,0:T(8,128)S(1)}, bf16[8,128,128]{2,1,0:T(8,128)(2,1)S(1)}) custom-call(s32[24]{0:T(128)S(1)} %get-tuple-element.25.rows_in, s32[24]{0:T(128)S(1)} %get-tuple-element.26.cols_in, s32[8,128]{1,0:T(8,128)S(1)} %get-tuple-element.27.count_in, bf16[2,1040,128]{2,1,0:T(8,128)(2,1)S(1)} %bitcast.8, ...), custom_call_target="tpu_custom_call" | custom-call | flops 402653184 | bytes 3145728 | tf_op jit(solution)/shard_map/pallas_call | solution.py:22
  82.4 2.2 %all-gather.4 = bf16[16,128,128]{2,1,0:T(8,128)(2,1)S(1)} all-gather(bf16[8,128,128]{2,1,0:T(8,128)(2,1)S(1)} %get-tuple-element.42), channel_id=6, replica_groups=mesh['row'=8,'col'=32,'rep'=2] {'rep'}, dimensions={0}, use_global_device_ids=true | all-gather | bytes 786432 | tf_op jit(solution)/shard_map/all_gather | solution.py:377
  84.7 0.1 shard_map.145
  84.8 14.0 %all_to_all.27.parts = bf16[8,160,128]{2,1,0:T(8,128)(2,1)S(1)} all-to-all(bf16[8,160,128]{2,1,0:T(8,128)(2,1)S(1)} %shard_map.145), channel_id=1, replica_groups=mesh['row'=8,'col'=32,'rep'=2] {'row'}, dimensions={0} | all-to-all | bytes 655360 | tf_op jit(solution)/shard_map/all_to_all | solution.py:268
  98.8 17.9 %all_to_all.28.gathered = bf16[32,32,128]{2,1,0:T(8,128)(2,1)S(1)} all-to-all(bf16[32,32,128]{2,1,0:T(8,128)(2,1)S(1)} %shard_map.146), channel_id=1, replica_groups=mesh['row'=8,'col'=32,'rep'=2] {'col'}, dimensions={0} | all-to-all | bytes 524288 | tf_op jit(solution)/shard_map/all_to_all | solution.py:268
  116.7 0.9 shard_map.147
  (2 shorter events, 0.1 us)
Async XLA Ops:
  2.2 20.4 %all-to-all-start = ((bf16[8,128,128]{2,1,0:T(8,128)(2,1)}), bf16[8,128,128]{2,1,0:T(8,128)(2,1)}, u32[]{:S(2)}, u32[]{:S(2)}) async-start(bf16[8,128,128]{2,1,0:T(8,128)(2,1)} %shard_map.138), calls=%async_computation | async-start | bytes 524288 | tf_op jit(solution)/shard_map/all_to_all | solution.py:268
  15.2 0.6 copy-start
  15.8 0.6 copy-start.2
  16.4 0.6 copy-start.4
  17.1 0.6 copy-start.6
  26.7 29.1 %copy-start.1 = (f32[32,512]{1,0:T(8,128)S(1)}, f32[32,512]{1,0:T(8,128)}, u32[]{:S(2)}) copy-start(f32[32,512]{1,0:T(8,128)} %copy-done) | copy-start | bytes 196612
  26.7 29.1 %copy-start.3 = (bf16[128,32]{1,0:T(8,128)(2,1)S(1)}, bf16[128,32]{1,0:T(8,128)(2,1)}, u32[]{:S(2)}) copy-start(bf16[128,32]{1,0:T(8,128)(2,1)} %copy-done.2) | copy-start | bytes 24580
  26.7 29.1 %copy-start.5 = (bf16[1,32,512]{2,1,0:T(8,128)(2,1)S(1)}, bf16[1,32,512]{2,1,0:T(8,128)(2,1)}, u32[]{:S(2)}) copy-start(bf16[1,32,512]{2,1,0:T(8,128)(2,1)} %copy-done.4) | copy-start | bytes 98308
  26.7 29.1 %copy-start.7 = (f32[32,1]{1,0:T(8,128)S(1)}, f32[32,1]{1,0:T(8,128)}, u32[]{:S(2)}) copy-start(f32[32,1]{1,0:T(8,128)} %copy-done.6) | copy-start | bytes 388
